TPU v7x, 32 devices: a whole 2x2x4 slice. The times are simulated.
32 devices in a mesh: dp: 4 (over y, x), tensor: 8 (over z, core).
Axes of the slice: x: 2, y: 2, z: 4, core: 2. Of those that a mesh axis runs over, the one named last changes fastest.
Arguments:
- tokens: bfloat16 [8, 1024, 1024], P(None, 'dp'), may hold values from -6 to 6
- cotangent: bfloat16 [8, 1024, 1024], P(None, 'dp'), may hold values from -6 to 6
- lengths: int32 [8], replicated, may hold values from 256 to 1024, as said below
- seq_deal: int32 [8], replicated, may hold values from 0 to 7, as said below
- norm_gains: bfloat16 [2, 2, 1024], replicated, may hold values from 0.5 to 1.5
- norm_shifts: bfloat16 [2, 2, 1024], replicated, may hold values from -2 to 2
- qkv_weight: bfloat16 [2, 1024, 3072], P(None, None, 'tensor'), may hold values from -0.1875 to 0.1875
- qkv_bias: bfloat16 [2, 3072], P(None, 'tensor'), may hold values from -2 to 2
- out_weight: bfloat16 [2, 1024, 1024], P(None, 'tensor'), may hold values from -0.5 to 0.5
- proj_bias: bfloat16 [2, 2, 1024], replicated, may hold values from -2 to 2
- up_weight: bfloat16 [2, 1024, 4096], P(None, None, 'tensor'), may hold values from -0.1875 to 0.1875
- up_bias: bfloat16 [2, 4096], P(None, 'tensor'), may hold values from -2 to 2
- down_weight: bfloat16 [2, 4096, 1024], P(None, 'tensor'), may hold values from -0.09375 to 0.09375
Outputs:
- activations: bfloat16 [8, 4, 256, 1024], P('dp', None, 'tensor')
- input_grad: bfloat16 [8, 1024, 1024], P(None, 'dp')
- grad_gains: float32 [2, 2, 1024], replicated
- grad_shifts: float32 [2, 2, 1024], replicated
- grad_qkv_weight: float32 [2, 1024, 3072], P(None, None, 'tensor')
- grad_qkv_bias: float32 [2, 3072], P(None, 'tensor')
- grad_out_weight: float32 [2, 1024, 1024], P(None, 'tensor')
- grad_proj_bias: float32 [2, 2, 1024], replicated
- grad_up_weight: float32 [2, 1024, 4096], P(None, None, 'tensor')
- grad_up_bias: float32 [2, 4096], P(None, 'tensor')
- grad_down_weight: float32 [2, 4096, 1024], P(None, 'tensor')
Inputs may be any that keep to these rules, and one draw needn't show every extreme that they name: `lengths`: at least one sequence has exactly 1024 tokens. `seq_deal`: A permutation of the sequence numbers; slots m = j * 2 to (j + 1) * 2 - 1 belong to index j of dp.
All inputs are finite; a program needn't handle non-finite values.
Results may differ from a plain program's by a relative error of at most 0.028.
Values may be sent and summed in bfloat16 or wider, within the bound.
No kernel may reach another device: no remote copies, remote signals or barrier semaphores. Data moves between devices by JAX's collectives and lax.ppermute only.
A program may use at most 192 MiB of HBM per device.

v0:
```python
from functools import partial

import jax
import jax.numpy as jnp
from jax import lax
from jax.sharding import PartitionSpec as P

HEADS = 16
LAYERS = 2


epsilon = 1e-05


def layer_norm(values, gain_row, shift_row):
    center = values - jnp.mean(values, -1, keepdims=True)
    variance = jnp.mean(center * center, -1, keepdims=True)
    return center * lax.rsqrt(variance + epsilon) * gain_row + shift_row


def gelu_tanh(values):
    return jax.nn.gelu(values, approximate=True)


def inner_rows(left_side, right_side):
    return lax.dot_general(
        left_side, right_side, (((0,), (0,)), ((), ())), preferred_element_type=jnp.float32
    )


def times_back(left_side, right_side):
    return lax.dot_general(
        left_side, right_side, (((1,), (1,)), ((), ())), preferred_element_type=jnp.float32
    )


def score_table(queries, key_rows, length, slopes):
    seq_len = queries.shape[0]
    scaling = queries.shape[2] ** (-0.5)
    row_index = jnp.arange(seq_len)[:, None]
    col_index = jnp.arange(seq_len)[None, :]
    scores = (
        jnp.einsum("qhd,khd->hqk", queries, key_rows, preferred_element_type=jnp.float32) * scaling
    )
    scores = scores + slopes[:, None, None] * (col_index - row_index).astype(jnp.float32)
    allowed = (col_index <= row_index) & (col_index < length)
    return jnp.where(allowed[None], scores, -1e30)


def attend_forward(packed, slopes):
    queries, key_rows, values, length = packed
    scores = score_table(queries, key_rows, length, slopes)
    highest = jnp.max(scores, -1, keepdims=True)
    log_total = highest + jnp.log(jnp.sum(jnp.exp(scores - highest), -1, keepdims=True))
    weights = jnp.exp(scores - log_total).astype(jnp.bfloat16)
    context = jnp.einsum("hqk,khd->qhd", weights, values, preferred_element_type=jnp.float32)
    return (context.astype(jnp.bfloat16), log_total)


def attend_backward(packed, slopes):
    queries, key_rows, values, length, log_total, context_grad = packed
    scaling = queries.shape[2] ** (-0.5)
    weights = jnp.exp(score_table(queries, key_rows, length, slopes) - log_total)
    weight_grad = jnp.einsum(
        "qhd,khd->hqk", context_grad, values, preferred_element_type=jnp.float32
    )
    value_grad = jnp.einsum(
        "hqk,qhd->khd",
        weights.astype(jnp.bfloat16),
        context_grad,
        preferred_element_type=jnp.float32,
    )
    center = jnp.sum(weight_grad * weights, -1, keepdims=True)
    score_grad = (weights * (weight_grad - center)).astype(jnp.bfloat16)
    query_grad = (
        jnp.einsum("hqk,khd->qhd", score_grad, key_rows, preferred_element_type=jnp.float32)
        * scaling
    )
    key_grad = (
        jnp.einsum("hqk,qhd->khd", score_grad, queries, preferred_element_type=jnp.float32)
        * scaling
    )
    return jnp.stack([query_grad, key_grad, value_grad], 2).astype(jnp.bfloat16)


def body(
    tokens,
    cotangent,
    lengths,
    seq_deal,
    norm_gains,
    norm_shifts,
    qkv_weight,
    qkv_bias,
    out_weight,
    proj_bias,
    up_weight,
    up_bias,
    down_weight,
):
    data_size = lax.axis_size("dp")
    tensor_size = lax.axis_size("tensor")
    data_rank = lax.axis_index("dp")
    tensor_rank = lax.axis_index("tensor")
    seq_total, held_len, features = tokens.shape
    seq_here = seq_total // data_size
    share_len = held_len // tensor_size
    seq_len = held_len * data_size
    head_dim = features // HEADS
    head_here = qkv_weight.shape[2] // (3 * head_dim)
    pieces = tuple(
        (
            jnp.take(
                lax.dynamic_slice_in_dim(member, tensor_rank * share_len, share_len, 1),
                seq_deal,
                axis=0,
            )
            for member in (tokens, cotangent)
        )
    )
    arrived = (
        lax.all_to_all(pieces[0], "dp", split_axis=0, concat_axis=1, tiled=True),
        lax.all_to_all(pieces[1], "dp", split_axis=0, concat_axis=1, tiled=True),
    )
    arrived = tuple(
        (member.reshape(seq_here, data_size, share_len, features) for member in arrived)
    )
    own_lengths = lax.dynamic_slice_in_dim(
        jnp.take(lengths, seq_deal), data_rank * seq_here, seq_here
    )
    position = (
        jnp.arange(data_size)[:, None] * held_len
        + tensor_rank * share_len
        + jnp.arange(share_len)[None, :]
    )
    keep_rows = (position[None] < own_lengths[:, None, None]).astype(jnp.float32).reshape(-1, 1)
    residual = arrived[0].reshape(-1, features).astype(jnp.float32) * keep_rows
    upstream = arrived[1].reshape(-1, features).astype(jnp.float32) * keep_rows
    head_ids = tensor_rank * head_here + jnp.arange(head_here)
    slopes = jnp.exp2(-8.0 * (head_ids + 1).astype(jnp.float32) / HEADS)
    full_up, full_down, full_upb = (up_weight, down_weight, up_bias)

    def spread(shard_rows):
        fourfold = shard_rows.reshape(seq_here, data_size, share_len, features)
        return lax.all_gather(fourfold, "tensor", axis=2, tiled=True).reshape(
            seq_here * seq_len, features
        )

    def collect(summand):
        fourfold = summand.reshape(seq_here, data_size, tensor_size * share_len, features)
        return (
            lax.psum_scatter(
                fourfold.astype(jnp.bfloat16), "tensor", scatter_dimension=2, tiled=True
            )
            .astype(jnp.float32)
            .reshape(-1, features)
        )

    def spread_back(shard_rows):
        fourfold = shard_rows.reshape(seq_here, data_size, share_len, features)
        return lax.all_gather(fourfold, "tensor", axis=2, tiled=True).reshape(
            seq_here * seq_len, features
        )

    def collect_back(summand):
        fourfold = summand.reshape(seq_here, data_size, tensor_size * share_len, features)
        return (
            lax.psum_scatter(
                fourfold.astype(jnp.bfloat16), "tensor", scatter_dimension=2, tiled=True
            )
            .astype(jnp.float32)
            .reshape(-1, features)
        )

    saved_layers = []
    for layer_index in range(LAYERS):
        gain_pair = norm_gains[layer_index].astype(jnp.float32)
        shift_pair = norm_shifts[layer_index].astype(jnp.float32)
        bias_pair = proj_bias[layer_index].astype(jnp.float32)
        first_norm = spread(layer_norm(residual, gain_pair[0], shift_pair[0]).astype(jnp.bfloat16))
        mixed_rows = jnp.dot(
            first_norm, qkv_weight[layer_index], preferred_element_type=jnp.float32
        ) + qkv_bias[layer_index].astype(jnp.float32)
        heads_view = mixed_rows.astype(jnp.bfloat16).reshape(
            seq_here, seq_len, head_here, 3, head_dim
        )
        context, log_totals = lax.map(
            partial(attend_forward, slopes=slopes),
            (heads_view[:, :, :, 0], heads_view[:, :, :, 1], heads_view[:, :, :, 2], own_lengths),
        )
        context = context.reshape(-1, head_here * head_dim)
        middle = residual + (
            collect(jnp.dot(context, out_weight[layer_index], preferred_element_type=jnp.float32))
            + bias_pair[0]
        )
        second_norm = spread(layer_norm(middle, gain_pair[1], shift_pair[1]).astype(jnp.bfloat16))
        upward = jnp.dot(
            second_norm, full_up[layer_index], preferred_element_type=jnp.float32
        ) + full_upb[layer_index].astype(jnp.float32)
        activated = gelu_tanh(upward).astype(jnp.bfloat16)
        following = middle + (
            collect(jnp.dot(activated, full_down[layer_index], preferred_element_type=jnp.float32))
            + bias_pair[1]
        )
        saved_layers.append(
            (
                residual,
                first_norm,
                heads_view,
                log_totals,
                context,
                middle,
                second_norm,
                upward,
                activated,
            )
        )
        residual = following
    activations = (
        (residual * keep_rows)
        .astype(jnp.bfloat16)
        .reshape(seq_here, data_size, share_len, features)
    )
    grad_rows = upstream
    weight_sets = []
    norm_sets = []
    for layer_index in reversed(range(LAYERS)):
        (
            before,
            first_norm,
            heads_view,
            log_totals,
            context,
            middle,
            second_norm,
            upward,
            activated,
        ) = saved_layers[layer_index]
        gain_pair = norm_gains[layer_index].astype(jnp.float32)
        shift_pair = norm_shifts[layer_index].astype(jnp.float32)
        down_grad = grad_rows.astype(jnp.bfloat16)
        down_bias_grad = jnp.sum(down_grad, 0, dtype=jnp.float32)
        down_rows = spread_back(down_grad)
        grad_down = inner_rows(activated, down_rows)
        act_grad = times_back(down_rows, full_down[layer_index])
        up_grad = jax.vjp(gelu_tanh, upward)[1](act_grad)[0].astype(jnp.bfloat16)
        grad_up_bias = jnp.sum(up_grad, 0, dtype=jnp.float32)
        grad_up = inner_rows(second_norm, up_grad)
        norm_grad = collect_back(times_back(up_grad, full_up[layer_index]))
        norm_pull = jax.vjp(layer_norm, middle, gain_pair[1], shift_pair[1])[1]
        middle_add, second_gain, second_shift = norm_pull(norm_grad)
        grad_rows = grad_rows + middle_add
        attn_grad = grad_rows.astype(jnp.bfloat16)
        out_bias_grad = jnp.sum(attn_grad, 0, dtype=jnp.float32)
        attn_rows = spread_back(attn_grad)
        grad_out = inner_rows(context, attn_rows)
        context_grad = (
            times_back(attn_rows, out_weight[layer_index])
            .astype(jnp.bfloat16)
            .reshape(seq_here, seq_len, head_here, head_dim)
        )
        mixed_grad = lax.map(
            partial(attend_backward, slopes=slopes),
            (
                heads_view[:, :, :, 0],
                heads_view[:, :, :, 1],
                heads_view[:, :, :, 2],
                own_lengths,
                log_totals,
                context_grad,
            ),
        )
        mixed_grad = mixed_grad.reshape(-1, 3 * head_here * head_dim)
        grad_qkv_bias = jnp.sum(mixed_grad, 0, dtype=jnp.float32)
        grad_qkv = inner_rows(first_norm, mixed_grad)
        norm_grad = collect_back(times_back(mixed_grad, qkv_weight[layer_index]))
        norm_pull = jax.vjp(layer_norm, before, gain_pair[0], shift_pair[0])[1]
        before_add, first_gain, first_shift = norm_pull(norm_grad)
        grad_rows = grad_rows + before_add
        weight_sets.insert(0, (grad_qkv, grad_qkv_bias, grad_out, grad_up, grad_up_bias, grad_down))
        norm_sets.insert(
            0,
            (
                jnp.stack([first_gain, second_gain]),
                jnp.stack([first_shift, second_shift]),
                jnp.stack([out_bias_grad, down_bias_grad]),
            ),
        )
    stacked = [
        jnp.stack([weight_sets[layer_index][member] for layer_index in range(LAYERS)])
        for member in range(6)
    ]
    norm_stacked = [
        jnp.stack([norm_sets[layer_index][member] for layer_index in range(LAYERS)])
        for member in range(3)
    ]
    summed = (
        lax.psum(stacked[0].astype(jnp.bfloat16), "dp").astype(jnp.float32),
        lax.psum(stacked[1].astype(jnp.bfloat16), "dp").astype(jnp.float32),
        lax.psum(stacked[2].astype(jnp.bfloat16), "dp").astype(jnp.float32),
        lax.psum(stacked[3].astype(jnp.bfloat16), "dp").astype(jnp.float32),
        lax.psum(stacked[4].astype(jnp.bfloat16), "dp").astype(jnp.float32),
        lax.psum(stacked[5].astype(jnp.bfloat16), "dp").astype(jnp.float32),
    )
    norm_summed = lax.psum((norm_stacked[0], norm_stacked[1], norm_stacked[2]), ("dp", "tensor"))
    home_rows = (
        (grad_rows * keep_rows)
        .astype(jnp.bfloat16)
        .reshape(seq_here, data_size, share_len, features)
    )
    returned = lax.all_to_all(home_rows, "dp", split_axis=1, concat_axis=0, tiled=True)
    returned = lax.all_gather(
        returned.reshape(seq_total, share_len, features), "tensor", axis=1, tiled=True
    )
    input_grad = jnp.take(returned, jnp.argsort(seq_deal), axis=0)
    return (
        activations,
        input_grad,
        norm_summed[0],
        norm_summed[1],
        summed[0],
        summed[1],
        summed[2],
        norm_summed[2],
        summed[3],
        summed[4],
        summed[5],
    )


def solution(mesh):
    placed = (
        P(None, "dp", None),
        P(None, "dp", None),
        P(),
        P(),
        P(),
        P(),
        P(None, None, "tensor"),
        P(None, "tensor"),
        P(None, "tensor", None),
        P(),
        P(None, None, "tensor"),
        P(None, "tensor"),
        P(None, "tensor", None),
    )
    return jax.shard_map(
        body,
        mesh=mesh,
        in_specs=placed,
        out_specs=(
            P("dp", None, "tensor", None),
            P(None, "dp", None),
            P(),
            P(),
            P(None, None, "tensor"),
            P(None, "tensor"),
            P(None, "tensor", None),
            P(),
            P(None, None, "tensor"),
            P(None, "tensor"),
            P(None, "tensor", None),
        ),
        check_vma=False,
    )
```

profile of v0, /device:TPU:0, one launch (start us, length us, event | category | flops | bytes accessed | tf_op | source)
XLA Modules:
  0.0 1322.3 jit_solution(877165915400309492)
XLA Ops:
  39.6 47.5 %all-gather.10.cloned.1.call-done = bf16[2,4,256,1024]{3,2,1,0:T(8,128)(2,1)} async-done(((bf16[2,4,32,1024]{3,2,1,0:T(8,128)(2,1)}), bf16[2,4,256,1024]{3,2,1,0:T(8,128)(2,1)}) %all-gather.10.cloned.1.call-update) | async-done | bytes 4194320 | tf_op jit(solution)/shard_map/all_gather | solution.py:145
  100.3 26.1 %while.48 = (s32[]{:T(128)}, bf16[2,1024,2,64]{1,3,2,0:T(8,128)(2,1)S(1)}, f32[2,2,1024,1]{2,1,3,0:T(2,128)S(1)}, bf16[2,1024,2,64]{1,3,2,0:T(8,128)(2,1)}, s32[...) while((s32[]{:T(128)}, ...), condition=%wide.region_5.7_spmd.clone, body=%wide.region_2.0_spmd.clone.sunk | while | flops 576846848 | bytes 47256212 | solution.py:187
  130.9 48.8 %reduce-scatter.9.cloned.1.call-done = bf16[2,4,32,1024]{3,2,1,0:T(8,128)(2,1)} async-done(((bf16[2,4,256,1024]{3,2,1,0:T(8,128)(2,1)}), bf16[2,4,32,1024]{3,2,1,0:T(8,128)(2,1)}) %reduce-scatter.9.cloned.1.call-update) | async-done | bytes 524304 | tf_op jit(solution)/shard_map/reduce_scatter | solution.py:152
  182.7 45.1 %all-gather.12.cloned.1.call-done = bf16[2,4,256,1024]{3,2,1,0:T(8,128)(2,1)} async-done(((bf16[2,4,32,1024]{3,2,1,0:T(8,128)(2,1)}), bf16[2,4,256,1024]{3,2,1,0:T(8,128)(2,1)}) %all-gather.12.cloned.1.call-update) | async-done | bytes 4194320 | tf_op jit(solution)/shard_map/all_gather | solution.py:145
  241.7 48.8 %reduce-scatter.11.cloned.1.call-done = bf16[2,4,32,1024]{3,2,1,0:T(8,128)(2,1)} async-done(((bf16[2,4,256,1024]{3,2,1,0:T(8,128)(2,1)}), bf16[2,4,32,1024]{3,2,1,0:T(8,128)(2,1)}) %reduce-scatter.11.cloned.1.call-update) | async-done | bytes 524304 | tf_op jit(solution)/shard_map/reduce_scatter | solution.py:152
  293.2 45.4 %all-gather.14.cloned.1.call-done = bf16[2,4,256,1024]{3,2,1,0:T(8,128)(2,1)} async-done(((bf16[2,4,32,1024]{3,2,1,0:T(8,128)(2,1)}), bf16[2,4,256,1024]{3,2,1,0:T(8,128)(2,1)}) %all-gather.14.cloned.1.call-update) | async-done | bytes 4194320 | tf_op jit(solution)/shard_map/all_gather | solution.py:145
  351.8 26.1 %while.49 = (s32[]{:T(128)}, bf16[2,1024,2,64]{1,3,2,0:T(8,128)(2,1)S(1)}, f32[2,2,1024,1]{2,1,3,0:T(2,128)S(1)}, bf16[2,1024,2,64]{1,3,2,0:T(8,128)(2,1)}, s32[...) while((s32[]{:T(128)}, ...), condition=%wide.region_15.17_spmd.clone, body=%wide.region_12.16_spmd.clone.sunk | while | flops 576846848 | bytes 47256212 | solution.py:187
  381.7 48.8 %reduce-scatter.13.cloned.1.call-done = bf16[2,4,32,1024]{3,2,1,0:T(8,128)(2,1)} async-done(((bf16[2,4,256,1024]{3,2,1,0:T(8,128)(2,1)}), bf16[2,4,32,1024]{3,2,1,0:T(8,128)(2,1)}) %reduce-scatter.13.cloned.1.call-update) | async-done | bytes 524304 | tf_op jit(solution)/shard_map/reduce_scatter | solution.py:152
  433.9 10.2 reduce-scatter.17.cloned.1.call-start
  444.0 34.5 %all-gather.16.cloned.1.call-done = bf16[2,4,256,1024]{3,2,1,0:T(8,128)(2,1)} async-done(((bf16[2,4,32,1024]{3,2,1,0:T(8,128)(2,1)}), bf16[2,4,256,1024]{3,2,1,0:T(8,128)(2,1)}) %all-gather.16.cloned.1.call-update) | async-done | bytes 4194320 | tf_op jit(solution)/shard_map/all_gather | solution.py:145
  478.6 8.6 multiply_convert_fusion.2
  487.2 39.5 %all-gather.18.cloned.1.call-done = bf16[2,4,256,1024]{3,2,1,0:T(8,128)(2,1)} async-done(((bf16[2,4,32,1024]{3,2,1,0:T(8,128)(2,1)}), bf16[2,4,256,1024]{3,2,1,0:T(8,128)(2,1)}) %all-gather.18.cloned.1.call-update) | async-done | bytes 4194320 | tf_op jit(solution)/shard_map/all_gather | solution.py:161
  526.7 9.7 fusion.213
  548.4 42.5 %reduce-scatter.17.cloned.1.call-done = bf16[2,4,32,1024]{3,2,1,0:T(8,128)(2,1)} async-done(((bf16[2,4,256,1024]{3,2,1,0:T(8,128)(2,1)}), bf16[2,4,32,1024]{3,2,1,0:T(8,128)(2,1)}) %reduce-scatter.17.cloned.1.call-update) | async-done | bytes 524304 | tf_op jit(solution)/shard_map/reduce_scatter | solution.py:168
  595.3 46.6 %reduce-scatter.15.cloned.1.call-done = bf16[2,4,32,1024]{3,2,1,0:T(8,128)(2,1)} async-done(((bf16[2,4,256,1024]{3,2,1,0:T(8,128)(2,1)}), bf16[2,4,32,1024]{3,2,1,0:T(8,128)(2,1)}) %reduce-scatter.15.cloned.1.call-update) | async-done | bytes 524304 | tf_op jit(solution)/shard_map/reduce_scatter | solution.py:152
  646.1 45.0 %all-gather.20.cloned.1.call-done = bf16[2,4,256,1024]{3,2,1,0:T(8,128)(2,1)} async-done(((bf16[2,4,32,1024]{3,2,1,0:T(8,128)(2,1)}), bf16[2,4,256,1024]{3,2,1,0:T(8,128)(2,1)}) %all-gather.20.cloned.1.call-update) | async-done | bytes 4194320 | tf_op jit(solution)/shard_map/all_gather | solution.py:161
  695.9 56.6 %while.50 = (s32[]{:T(128)}, bf16[2,1024,2,3,64]{1,4,2,3,0:T(8,128)(2,1)S(1)}, bf16[2,1024,2,64]{1,3,2,0:T(8,128)(2,1)}, s32[2]{0:T(128)S(1)}, bf16[2,1024,2,64]...) while((s32[]{:T(128)}, ...), condition=%wide.region_26.28_spmd.clone, body=%wide.region_24.27_spmd.clone.sunk | while | flops 1372453888 | bytes 111194296 | solution.py:262
  711.8 8.1 multiply_convert_fusion.8
  740.1 8.1 multiply_convert_fusion.8
  764.1 48.8 %reduce-scatter.19.cloned.1.call-done = bf16[2,4,32,1024]{3,2,1,0:T(8,128)(2,1)} async-done(((bf16[2,4,256,1024]{3,2,1,0:T(8,128)(2,1)}), bf16[2,4,32,1024]{3,2,1,0:T(8,128)(2,1)}) %reduce-scatter.19.cloned.1.call-update) | async-done | bytes 524304 | tf_op jit(solution)/shard_map/reduce_scatter | solution.py:168
  820.2 45.4 %all-gather.22.cloned.1.call-done = bf16[2,4,256,1024]{3,2,1,0:T(8,128)(2,1)} async-done(((bf16[2,4,32,1024]{3,2,1,0:T(8,128)(2,1)}), bf16[2,4,256,1024]{3,2,1,0:T(8,128)(2,1)}) %all-gather.22.cloned.1.call-update) | async-done | bytes 4194320 | tf_op jit(solution)/shard_map/all_gather | solution.py:161
  865.6 9.6 fusion.214
  881.0 48.8 %reduce-scatter.21.cloned.1.call-done = bf16[2,4,32,1024]{3,2,1,0:T(8,128)(2,1)} async-done(((bf16[2,4,256,1024]{3,2,1,0:T(8,128)(2,1)}), bf16[2,4,32,1024]{3,2,1,0:T(8,128)(2,1)}) %reduce-scatter.21.cloned.1.call-update) | async-done | bytes 524304 | tf_op jit(solution)/shard_map/reduce_scatter | solution.py:168
  937.9 45.4 %all-gather.24.cloned.1.call-done = bf16[2,4,256,1024]{3,2,1,0:T(8,128)(2,1)} async-done(((bf16[2,4,32,1024]{3,2,1,0:T(8,128)(2,1)}), bf16[2,4,256,1024]{3,2,1,0:T(8,128)(2,1)}) %all-gather.24.cloned.1.call-update) | async-done | bytes 4194320 | tf_op jit(solution)/shard_map/all_gather | solution.py:161
  988.6 56.6 %while.51 = (s32[]{:T(128)}, bf16[2,1024,2,3,64]{1,4,2,3,0:T(8,128)(2,1)S(1)}, bf16[2,1024,2,64]{1,3,2,0:T(8,128)(2,1)}, s32[2]{0:T(128)S(1)}, bf16[2,1024,2,64]...) while((s32[]{:T(128)}, ...), condition=%wide.region_35.37_spmd.clone, body=%wide.region_33.36_spmd.clone.sunk | while | flops 1372453888 | bytes 111194296 | solution.py:262
  1004.5 8.1 multiply_convert_fusion.9
  1032.8 8.1 multiply_convert_fusion.9
  1088.5 16.8 %reduce-scatter.23.cloned.1.call-done = bf16[2,4,32,1024]{3,2,1,0:T(8,128)(2,1)} async-done(((bf16[2,4,256,1024]{3,2,1,0:T(8,128)(2,1)}), bf16[2,4,32,1024]{3,2,1,0:T(8,128)(2,1)}) %reduce-scatter.23.cloned.1.call-update) | async-done | bytes 524304 | tf_op jit(solution)/shard_map/reduce_scatter | solution.py:168
  1110.6 16.3 %all_to_all.33 = bf16[2,4,32,1024]{3,2,0,1:T(8,128)(2,1)} all-to-all(bf16[2,4,32,1024]{3,2,0,1:T(8,128)(2,1)S(1)} %copy.115), channel_id=1, replica_groups=mesh['dp'=4,'tensor'=8] {'dp'}, dimensions={1} | all-to-all | bytes 1048576 | tf_op jit(solution)/shard_map/all_to_all | solution.py:311
  1130.3 9.2 all-reduce.1
  1140.7 111.0 %all-reduce.5.cloned.1.call-done = (bf16[2,1024,384]{2,1,0:T(8,128)(2,1)}, bf16[2,128,1024]{2,1,0:T(8,128)(2,1)}, bf16[2,1024,512]{2,1,0:T(8,128)(2,1)}, bf16[2,512,1024]{2,1,0:T(8,128)(2,1)}) async-done(((bf16[2,1024,384]{2,1,0:T(8,128)(2,1)}, bf16[2,128,1024]{2,1,0:T(8,128)(2,1)}, bf16[2,1024,512]{2,1,0:T(8,128)(2,1)}, bf16[2,512,1024]{2,1,0:T(8,128)(2,1)}), (bf16[2,1024,384]{2,1,0:T(8,128)(2,1)}, ...) | async-done | bytes 6291472 | tf_op jit(solution)/shard_map/psum | solution.py:298
  1262.4 43.0 %all-reduce = (f32[2,2,1024]{2,1,0:T(2,128)}, f32[2,2,1024]{2,1,0:T(2,128)}, f32[2,2,1024]{2,1,0:T(2,128)}) all-reduce(f32[2,2,1024]{2,1,0:T(2,128)S(1)} %pad_maximum_fusion.4, f32[2,2,1024]{2,1,0:T(2,128)S(1)} %pad_maximum_fusion.5, f32[2,2,1024]{2,1,0:T(2,128)S(1)} %pad_maximum_fusion.6), channel_id=1, replica_groups=mesh['dp'=4,'tensor'=8] {'dp','tensor'}, use_global_device_ids=true, to_apply=%region_43.45 | all-reduce | flops 12288 | bytes 98304 | tf_op jit(solution)/shard_map/psum | solution.py:305
  (472 shorter events, 358.0 us)
Async XLA Ops:
  12.8 13.2 all-to-all-start
  18.8 162.5 %copy-start.44 = (f32[1,1,1024]{2,1,0:T(1,128)}, f32[1,1,1024]{2,1,0:T(1,128)S(1)}, u32[]{:S(2)}) copy-start(f32[1,1,1024]{2,1,0:T(1,128)S(1)} %get-tuple-element.536) | copy-start | bytes 12292
  18.8 273.3 %copy-start.38 = (f32[1,1,1024]{2,1,0:T(1,128)}, f32[1,1,1024]{2,1,0:T(1,128)S(1)}, u32[]{:S(2)}) copy-start(f32[1,1,1024]{2,1,0:T(1,128)S(1)} %get-tuple-element.501) | copy-start | bytes 12292
  18.9 623.0 %copy-start.28 = (f32[2,4,32]{2,1,0:T(4,128)}, f32[2,4,32]{2,1,0:T(4,128)S(1)}, u32[]{:S(2)}) copy-start(f32[2,4,32]{2,1,0:T(4,128)S(1)} %compare_convert_fusion) | copy-start | bytes 3076
  26.0 10.6 all-to-all-start.1
  29.5 57.6 %all-gather.10.cloned.1.call-start = ((), (), s32[]{:S(2)}) async-start(), calls=%async_computation.11 | async-start | bytes 4718592 | tf_op jit(solution)/shard_map/all_gather | solution.py:145
  29.7 150.0 %copy-start.8 = (f32[4,2,32,1024]{3,2,1,0:T(8,128)}, f32[4,2,32,1024]{3,2,1,0:T(8,128)S(1)}, u32[]{:S(2)}) copy-start(f32[4,2,32,1024]{3,2,1,0:T(8,128)S(1)} %bitcast_convert_fusion) | copy-start | bytes 3145732
  29.9 57.2 %copy-start.34 = (f32[2,4,32]{2,1,0:T(4,128)}, f32[2,4,32]{2,1,0:T(4,128)S(1)}, u32[]{:S(2)}) copy-start(f32[2,4,32]{2,1,0:T(4,128)S(1)} %broadcast_multiply_fusion.3) | copy-start | bytes 3076
  30.2 56.9 %copy-start.51 = (f32[2,4,32]{2,1,0:T(4,128)}, f32[2,4,32]{2,1,0:T(4,128)S(1)}, u32[]{:S(2)}) copy-start(f32[2,4,32]{2,1,0:T(4,128)S(1)} %multiply_reduce_fusion.5) | copy-start | bytes 3076
  30.2 56.9 %copy-start.47 = (f32[2,4,32]{2,1,0:T(4,128)}, f32[2,4,32]{2,1,0:T(4,128)S(1)}, u32[]{:S(2)}) copy-start(f32[2,4,32]{2,1,0:T(4,128)S(1)} %fusion.197) | copy-start | bytes 3076
  39.5 140.1 %reduce-scatter.9.cloned.1.call-start = ((), (), s32[]{:S(2)}) async-start(), calls=%async_computation.12 | async-start | bytes 4718592 | tf_op jit(solution)/shard_map/reduce_scatter | solution.py:152
  130.8 97.0 %all-gather.12.cloned.1.call-start = ((), (), s32[]{:S(2)}) async-start(), calls=%async_computation.13 | async-start | bytes 4718592 | tf_op jit(solution)/shard_map/all_gather | solution.py:145
  181.0 109.5 %copy-start.6 = (f32[2,4,32,1024]{3,2,1,0:T(8,128)}, f32[2,4,32,1024]{3,2,1,0:T(8,128)S(1)}, u32[]{:S(2)}) copy-start(f32[2,4,32,1024]{3,2,1,0:T(8,128)S(1)} %get-tuple-element.480) | copy-start | bytes 3145732
  182.4 108.1 %reduce-scatter.11.cloned.1.call-start = ((), (), s32[]{:S(2)}) async-start(), calls=%async_computation.14 | async-start | bytes 4718592 | tf_op jit(solution)/shard_map/reduce_scatter | solution.py:152
  241.6 97.0 %all-gather.14.cloned.1.call-start = ((), (), s32[]{:S(2)}) async-start(), calls=%async_computation.15 | async-start | bytes 4718592 | tf_op jit(solution)/shard_map/all_gather | solution.py:145
  291.8 138.7 %copy-start.4 = (f32[2,4,32,1024]{3,2,1,0:T(8,128)}, f32[2,4,32,1024]{3,2,1,0:T(8,128)S(1)}, u32[]{:S(2)}) copy-start(f32[2,4,32,1024]{3,2,1,0:T(8,128)S(1)} %get-tuple-element.478) | copy-start | bytes 3145732
  293.2 137.3 %reduce-scatter.13.cloned.1.call-start = ((), (), s32[]{:S(2)}) async-start(), calls=%async_computation.16 | async-start | bytes 4718592 | tf_op jit(solution)/shard_map/reduce_scatter | solution.py:152
  381.6 97.0 %all-gather.16.cloned.1.call-start = ((), (), s32[]{:S(2)}) async-start(), calls=%async_computation.17 | async-start | bytes 4718592 | tf_op jit(solution)/shard_map/all_gather | solution.py:145
  433.1 93.5 %all-gather.18.cloned.1.call-start = ((), (), s32[]{:S(2)}) async-start(), calls=%async_computation.19 | async-start | bytes 4718592 | tf_op jit(solution)/shard_map/all_gather | solution.py:161
  433.9 157.1 %reduce-scatter.17.cloned.1.call-start = ((), (), s32[]{:S(2)}) async-start(), calls=%async_computation.20 | async-start | bytes 4718592 | tf_op jit(solution)/shard_map/reduce_scatter | solution.py:168
  542.1 99.8 %reduce-scatter.15.cloned.1.call-start = ((), (), s32[]{:S(2)}) async-start(), calls=%async_computation.18 | async-start | bytes 4718592 | tf_op jit(solution)/shard_map/reduce_scatter | solution.py:152
  548.3 93.5 %copy-start.16 = (f32[4,2,32,1024]{3,2,1,0:T(8,128)S(1)}, f32[4,2,32,1024]{3,2,1,0:T(8,128)}, u32[]{:S(2)}) copy-start(f32[4,2,32,1024]{3,2,1,0:T(8,128)} %copy-done.15) | copy-start | bytes 3145732
  548.4 142.7 %all-gather.20.cloned.1.call-start = ((), (), s32[]{:S(2)}) async-start(), calls=%async_computation.21 | async-start | bytes 4718592 | tf_op jit(solution)/shard_map/all_gather | solution.py:161
  645.6 167.3 %reduce-scatter.19.cloned.1.call-start = ((), (), s32[]{:S(2)}) async-start(), calls=%async_computation.22 | async-start | bytes 4718592 | tf_op jit(solution)/shard_map/reduce_scatter | solution.py:168
  757.9 55.1 %copy-start.5 = (f32[2,4,32,1024]{3,2,1,0:T(8,128)S(1)}, f32[2,4,32,1024]{3,2,1,0:T(8,128)}, u32[]{:S(2)}) copy-start(f32[2,4,32,1024]{3,2,1,0:T(8,128)} %copy-done.4) | copy-start | bytes 3145732
  764.0 101.5 %copy-start.74 = (f32[1,512]{1,0:T(1,128)S(1)}, f32[1,512]{1,0:T(1,128)}, u32[]{:S(2)}) copy-start(f32[1,512]{1,0:T(1,128)} %copy-done.73) | copy-start | bytes 6148
  764.0 101.5 %all-gather.22.cloned.1.call-start = ((), (), s32[]{:S(2)}) async-start(), calls=%async_computation.23 | async-start | bytes 4718592 | tf_op jit(solution)/shard_map/all_gather | solution.py:161
  820.1 109.7 %reduce-scatter.21.cloned.1.call-start = ((), (), s32[]{:S(2)}) async-start(), calls=%async_computation.24 | async-start | bytes 4718592 | tf_op jit(solution)/shard_map/reduce_scatter | solution.py:168
  881.0 102.4 %all-gather.24.cloned.1.call-start = ((), (), s32[]{:S(2)}) async-start(), calls=%async_computation.25 | async-start | bytes 4718592 | tf_op jit(solution)/shard_map/all_gather | solution.py:161
  937.9 167.5 %reduce-scatter.23.cloned.1.call-start = ((), (), s32[]{:S(2)}) async-start(), calls=%async_computation.26 | async-start | bytes 4718592 | tf_op jit(solution)/shard_map/reduce_scatter | solution.py:168
  1056.5 195.2 %all-reduce.5.cloned.1.call-start = ((), (), s32[]{:S(2)}) async-start(), calls=%async_computation.28 | async-start | bytes 12582912 | tf_op jit(solution)/shard_map/psum | solution.py:298
  1088.5 216.9 %all-gather.26.cloned.1.call-start = ((), (), s32[]{:S(2)}) async-start(), calls=%async_computation.27 | async-start | bytes 4718592 | tf_op jit(solution)/shard_map/all_gather | solution.py:312
  (84 other events, 1712.5 us)
Sparse Core Ops, SparseCore 0:
  39.6 47.4 all-gather.9
  130.9 48.7 reduce-scatter.8
  182.5 45.2 all-gather.11
  241.7 48.7 reduce-scatter.10
  293.3 45.2 all-gather.13
  381.7 48.7 reduce-scatter.12
  433.3 45.2 all-gather.15
  480.8 45.8 all-gather.17
  542.2 48.7 reduce-scatter.16
  593.7 48.1 reduce-scatter.14
  645.8 45.2 all-gather.19
  764.2 48.7 reduce-scatter.18
  820.2 45.2 all-gather.21
  881.1 48.7 reduce-scatter.20
  938.0 45.2 all-gather.23
  1056.6 48.7 reduce-scatter.22
  1110.1 141.5 all-reduce.4
  1253.1 48.0 all-gather.25
where the time goes:
time: 1330 us; the launch traced here: 1320 us
  waiting for transfers between devices  823 us (62%)
  matrix products  202 us (15%)
  other arithmetic  123 us (9%)
  local copies, waits for them, and re-layouts  69.3 us (5%)
  blocking collectives  68.5 us (5%)
  starting transfers between devices  20.3 us (2%)
  between operations  16 us (1%)
    reduce_scatter x4, waiting for transfers between devices, collect(): lax.psum_scatter(fourfold.astype(jnp.bfloat16), 'tensor', scatter_dimensi...  193 us
    all_gather x4, waiting for transfers between devices, spread_back(): lax.all_gather(fourfold, 'tensor', axis=2, tiled=True)  175 us
    all_gather x4, waiting for transfers between devices, spread(): lax.all_gather(fourfold, 'tensor', axis=2, tiled=True)  173 us
    reduce_scatter x4, waiting for transfers between devices, collect_back(): lax.psum_scatter(fourfold.astype(jnp.bfloat16), 'tensor', scatter_dimensi...  157 us
    psum x1, waiting for transfers between devices, body(): lax.psum(stacked[0].astype(jnp.bfloat16), 'dp').astype(jnp.float32)  111 us
    dot_general x8, matrix products, times_back(): lax.dot_general(left_side, right_side, (((1,), (1,)), ((), ())), preferre...  47.2 us
    psum x1, blocking collectives, body(): lax.psum((norm_stacked[0], norm_stacked[1], norm_stacked[2]), ('dp', 'ten...  43 us
    dot_general x8, matrix products, score_table(): jnp.einsum('qhd,khd->hqk', queries, key_rows, preferred_element_type=jnp....  34.7 us
  transfers between devices with their start and end apart: 20, of which 19 were waited for; matrix products, arithmetic and copies ran while one was open for 5% of the time, Pallas kernels for 0%

commit v1 on v0

v1 whole, which is shorter than its diff:
```python
import math

import jax
import jax.numpy as jnp
from jax import lax
from jax.sharding import PartitionSpec as P

HEADS = 16
LAYERS = 2
EPSILON = 1e-05
BF16 = jnp.bfloat16
F32 = jnp.float32


def dot(left_side, right_side, left_dim, right_dim):
    return lax.dot_general(
        left_side,
        right_side,
        (((left_dim,), (right_dim,)), ((), ())),
        preferred_element_type=F32,
    )


def norm_parts(values):
    center = values - jnp.mean(values, -1, keepdims=True)
    variance = jnp.mean(center * center, -1, keepdims=True)
    return center, lax.rsqrt(variance + EPSILON)


def layer_norm(values, gain_row, shift_row):
    center, inverse = norm_parts(values)
    return center * inverse * gain_row + shift_row


def norm_back(values, gain_row, norm_grad):
    center, inverse = norm_parts(values)
    unit = center * inverse
    scaled = norm_grad * gain_row
    gain_grad = jnp.sum(norm_grad * unit, 0)
    shift_grad = jnp.sum(norm_grad, 0)
    through = inverse * (
        scaled
        - jnp.mean(scaled, -1, keepdims=True)
        - unit * jnp.mean(scaled * unit, -1, keepdims=True)
    )
    return through, gain_grad, shift_grad


def gelu_pair(values):
    root = math.sqrt(2.0 / math.pi)
    square = values * values
    bend = jnp.tanh(root * values * (1.0 + 0.044715 * square))
    half = 0.5 * (1.0 + bend)
    slope = half + 0.5 * values * (1.0 - bend * bend) * root * (1.0 + 3 * 0.044715 * square)
    return values * half, slope


def score_table(queries, key_rows, slopes, position, length):
    scaling = queries.shape[2] ** (-0.5)
    scores = jnp.einsum("qhd,khd->hqk", queries, key_rows, preferred_element_type=F32) * scaling
    offset = (position[None, :] - position[:, None]).astype(F32)
    scores = scores + slopes[:, None, None] * offset
    allowed = (position[None, :] <= position[:, None]) & (position[None, :] < length)
    return jnp.where(allowed[None], scores, -1e30)


def attend_forward(queries, key_rows, values, slopes, position, length):
    scores = score_table(queries, key_rows, slopes, position, length)
    highest = jnp.max(scores, -1, keepdims=True)
    log_total = highest + jnp.log(jnp.sum(jnp.exp(scores - highest), -1, keepdims=True))
    weights = jnp.exp(scores - log_total).astype(BF16)
    context = jnp.einsum("hqk,khd->qhd", weights, values, preferred_element_type=F32)
    return context.astype(BF16), log_total


def attend_backward(queries, key_rows, values, slopes, position, length, log_total, context_grad):
    scaling = queries.shape[2] ** (-0.5)
    weights = jnp.exp(score_table(queries, key_rows, slopes, position, length) - log_total)
    weight_grad = jnp.einsum("qhd,khd->hqk", context_grad, values, preferred_element_type=F32)
    value_grad = jnp.einsum(
        "hqk,qhd->khd", weights.astype(BF16), context_grad, preferred_element_type=F32
    )
    center = jnp.sum(weight_grad * weights, -1, keepdims=True)
    score_grad = (weights * (weight_grad - center)).astype(BF16)
    query_grad = (
        jnp.einsum("hqk,khd->qhd", score_grad, key_rows, preferred_element_type=F32) * scaling
    )
    key_grad = (
        jnp.einsum("hqk,qhd->khd", score_grad, queries, preferred_element_type=F32) * scaling
    )
    return jnp.stack([query_grad, key_grad, value_grad], 1).astype(BF16)


def make_body(data_size, tensor_size):
    X = math.isqrt(data_size)
    Y = data_size // X
    C = 2
    Z = tensor_size // C
    OWN = Z // X

    def send(value, rule):
        pairs = []
        for y in range(Y):
            for x in range(X):
                for z in range(Z):
                    for c in range(C):
                        target = rule(y, x, z, c)
                        if target is not None:
                            ty, tx, tz, tc = target
                            pairs.append(
                                (
                                    ((y * X + x) * Z + z) * C + c,
                                    ((ty * X + tx) * Z + tz) * C + tc,
                                )
                            )
        return lax.ppermute(value, ("dp", "tensor"), pairs)

    def body(
        tokens,
        cotangent,
        lengths,
        seq_deal,
        norm_gains,
        norm_shifts,
        qkv_weight,
        qkv_bias,
        out_weight,
        proj_bias,
        up_weight,
        up_bias,
        down_weight,
    ):
        data_rank = lax.axis_index("dp")
        tensor_rank = lax.axis_index("tensor")
        y_at, x_at = data_rank // X, data_rank % X
        z_at, c_at = tensor_rank // C, tensor_rank % C
        seq_total, held_len, features = tokens.shape
        head_dim = features // HEADS
        group = X * C
        blocks = Y // C
        rows_here = blocks * held_len
        seq_len = rows_here * group
        is_owner = z_at // OWN == x_at

        def spread(rows):
            near = [rows] + [send(rows, lambda y, x, z, c: (y, x, z, (c + 1) % C))]
            pieces = list(near)
            for step in range(1, X):
                got = send(rows, lambda y, x, z, c: (y, (x - step) % X, z, c))
                pieces += [got, send(got, lambda y, x, z, c: (y, x, z, (c + 1) % C))]
            return jnp.concatenate(pieces, 0)

        def collect(left_side, weight, weight_dim):
            half_rows = C * rows_here
            total = None
            for step in list(range(1, X)) + [0]:
                part = dot(
                    left_side[step * half_rows : (step + 1) * half_rows], weight, 1, weight_dim
                ).astype(BF16)
                got = send(part[rows_here:], lambda y, x, z, c: (y, x, z, (c + 1) % C))
                part = part[:rows_here].astype(F32) + got.astype(F32)
                if step:
                    part = send(
                        part.astype(BF16), lambda y, x, z, c: (y, (x + step) % X, z, c)
                    ).astype(F32)
                total = part if total is None else total + part
            return total

        def fetch(piece):
            arrived = None
            for step in range(1, Z // OWN):
                got = send(
                    piece,
                    lambda y, x, z, c: (
                        (y, x, (z + OWN * step) % Z, c) if z // OWN == x else None
                    ),
                )
                arrived = got if arrived is None else arrived + got
            piece = jnp.where(is_owner, piece, arrived)
            shards = [piece] + [
                send(piece, lambda y, x, z, c: (y, x, z // OWN * OWN + (z - step) % OWN, c))
                for step in range(1, OWN)
            ]
            full = []
            for shard in shards:
                full.append(shard)
                for step in range(1, Y):
                    full.append(send(shard, lambda y, x, z, c: ((y - step) % Y, x, z, c)))
            return full

        def settle(parts, wire=BF16):
            sums = []
            for shard in range(OWN):
                here = parts[shard * Y].astype(F32)
                for step in range(1, Y):
                    here += send(
                        parts[shard * Y + step].astype(wire),
                        lambda y, x, z, c: ((y + step) % Y, x, z, c),
                    ).astype(F32)
                sums.append(here)
            here = sums[0]
            for step in range(1, OWN):
                here += send(
                    sums[step].astype(wire),
                    lambda y, x, z, c: (y, x, z // OWN * OWN + (z + step) % OWN, c),
                ).astype(F32)
            low = here.astype(wire)
            for step in range(1, Z // OWN):
                here += send(
                    low,
                    lambda y, x, z, c: (
                        (y, x, (z + OWN * step) % Z, c)
                        if ((z + OWN * step) % Z) // OWN == x
                        else None
                    ),
                ).astype(F32)
            low = here.astype(wire)
            arrived = None
            for step in range(1, X):
                got = send(
                    low,
                    lambda y, x, z, c: ((y, (x + step) % X, z, c) if z // OWN == x else None),
                )
                arrived = got if arrived is None else arrived + got
            low = jnp.where(is_owner, low, arrived)
            relative = [low] + [
                send(low, lambda y, x, z, c: ((y - step) % Y, x, z, c)) for step in range(1, Y)
            ]
            stacked = jnp.stack(relative)
            return jnp.roll(stacked, y_at, 0) if Y > 2 else jnp.where(
                y_at == 0, stacked, stacked[::-1]
            )

        def own_part(array, axis):
            size = array.shape[axis] // Y
            return lax.dynamic_slice_in_dim(array, y_at * size, size, axis)

        shard_heads = qkv_weight.shape[2] // (3 * head_dim)
        shard_width = shard_heads * head_dim
        weights = []
        bias_rows = []
        qkv_bias_view = (
            qkv_bias.reshape(LAYERS, shard_heads, 3, head_dim)
            .transpose(0, 2, 1, 3)
            .reshape(LAYERS, 3, shard_width)
        )
        qkv_bias_part = own_part(qkv_bias_view, 2).reshape(1, -1)
        up_bias_part = own_part(up_bias, 1).reshape(1, -1)
        bias_cut = qkv_bias_part.shape[1]
        bias_parts = fetch(jnp.concatenate([qkv_bias_part, up_bias_part], 1))
        full_qkv_bias = jnp.concatenate(
            [part[0, :bias_cut].reshape(LAYERS, 3, -1) for part in bias_parts], 2
        ).reshape(LAYERS, -1).astype(F32)
        full_up_bias = jnp.concatenate(
            [part[0, bias_cut:].reshape(LAYERS, -1) for part in bias_parts], 1
        ).astype(F32)
        for layer in range(LAYERS):
            qkv_view = (
                qkv_weight[layer]
                .reshape(features, shard_heads, 3, head_dim)
                .transpose(2, 1, 3, 0)
                .reshape(3, shard_width, features)
            )
            qkv_full = jnp.concatenate(fetch(own_part(qkv_view, 1)), 1).reshape(-1, features)
            out_full = jnp.concatenate(fetch(own_part(out_weight[layer], 0)), 0)
            up_full = jnp.concatenate(fetch(own_part(up_weight[layer], 1)), 1)
            down_full = jnp.concatenate(fetch(own_part(down_weight[layer], 0)), 0)
            weights.append((qkv_full, out_full, up_full, down_full))

        head_here = weights[0][1].shape[0] // head_dim
        part_width = shard_width // Y
        element = jnp.arange(head_here) * head_dim
        shard_step = element // shard_width
        y_step = element % shard_width // part_width
        shard_z = x_at * OWN + (z_at + shard_step) % OWN
        y_true = (y_at + y_step) % Y
        head_ids = ((shard_z * C + c_at) * shard_width + y_true * part_width) // head_dim
        slopes = jnp.exp2(-8.0 * (head_ids + 1).astype(F32) / HEADS)

        slot = y_at * Z + z_at
        sequence = seq_deal[slot]
        length = lengths[sequence]

        def deal(member):
            pieces = []
            for step in range(Y):
                target = (y_at + step) % Y
                picked = lax.dynamic_index_in_dim(
                    member, seq_deal[target * Z + z_at], 0, keepdims=False
                )
                if step:
                    picked = send(
                        picked,
                        lambda y, x, z, c: (
                            ((y + step) % Y, x, z, c) if y // blocks == c else None
                        ),
                    )
                pieces.append(picked)
            if Y == 2:
                return jnp.where(y_at == c_at, pieces[0], pieces[1])
            stacked = jnp.stack(pieces)
            wanted = (y_at - (c_at * blocks + jnp.arange(blocks))) % Y
            return jnp.take(stacked, wanted, axis=0).reshape(-1, features)

        def positions(x_of, c_of):
            block = (c_of * blocks + jnp.arange(blocks)) * X + x_of
            return (block[:, None] * held_len + jnp.arange(held_len)[None, :]).reshape(-1)

        own_position = positions(x_at, c_at)
        position = jnp.concatenate(
            [
                positions((x_at + x_step) % X, (c_at + c_step) % C)
                for x_step in range(X)
                for c_step in range(C)
            ]
        )
        keep_rows = (own_position < length).astype(F32)[:, None]
        residual = deal(tokens).astype(F32) * keep_rows
        grad_rows = deal(cotangent).astype(F32) * keep_rows

        def split_heads(rows):
            cut = rows.reshape(seq_len, 3, head_here, head_dim)
            return cut[:, 0], cut[:, 1], cut[:, 2]

        saved = []
        for layer in range(LAYERS):
            qkv_full, out_full, up_full, down_full = weights[layer]
            gains = norm_gains[layer].astype(F32)
            shifts = norm_shifts[layer].astype(F32)
            biases = proj_bias[layer].astype(F32)
            before = residual
            first_norm = spread(layer_norm(before, gains[0], shifts[0]).astype(BF16))
            mixed = (dot(first_norm, qkv_full, 1, 1) + full_qkv_bias[layer]).astype(BF16)
            context, log_total = attend_forward(*split_heads(mixed), slopes, position, length)
            context = context.reshape(seq_len, -1)
            middle = before + (collect(context, out_full, 0) + biases[0])
            second_norm = spread(layer_norm(middle, gains[1], shifts[1]).astype(BF16))
            upward = dot(second_norm, up_full, 1, 0) + full_up_bias[layer]
            activated, act_slope = gelu_pair(upward)
            activated = activated.astype(BF16)
            act_slope = act_slope.astype(BF16)
            residual = middle + (collect(activated, down_full, 0) + biases[1])
            saved.append(
                (
                    before,
                    first_norm,
                    mixed,
                    log_total,
                    context,
                    middle,
                    second_norm,
                    activated,
                    act_slope,
                )
            )

        final = (residual * keep_rows).astype(BF16)
        slots_dev = seq_total // (Y * X)
        moved = []
        for step in range(X):
            source = final
            if step:
                source = send(
                    final,
                    lambda y, x, z, c: (
                        (y, (x + step) % X, z, c) if (x + step) % X == z // slots_dev else None
                    ),
                )
            moved.append(source)
        moved = jnp.stack(moved)
        order = (x_at - jnp.arange(X)) % X
        moved = jnp.take(moved, order, axis=0)
        share = held_len // tensor_size
        moved = moved.reshape(X, blocks, Z, C, share, features)
        by_z = []
        for step in range(Z):
            outgoing = lax.dynamic_index_in_dim(moved, (z_at + step) % Z, 2, keepdims=False)
            if step:
                outgoing = send(
                    outgoing,
                    lambda y, x, z, c: (
                        (y, x, (z + step) % Z, c) if z // slots_dev == x else None
                    ),
                )
            by_z.append(outgoing)
        by_z = jnp.stack(by_z)
        wanted = (z_at - (x_at * slots_dev + jnp.arange(slots_dev))) % Z
        mine = jnp.take(by_z, wanted, axis=0)
        kept = lax.dynamic_index_in_dim(mine, c_at, 3, keepdims=False)
        given = lax.dynamic_index_in_dim(mine, 1 - c_at, 3, keepdims=False)
        given = send(given, lambda y, x, z, c: (y, x, z, (c + 1) % C))
        both = jnp.where(
            c_at == 0, jnp.stack([kept, given], 2), jnp.stack([given, kept], 2)
        )
        activations = both.transpose(0, 2, 3, 1, 4, 5).reshape(
            slots_dev, Y * X, share, features
        )

        outputs = [None] * LAYERS
        small = [None] * LAYERS
        bias_grads = [None] * LAYERS

        def cut_rows(array, pieces):
            size = array.shape[0] // pieces
            return [array[at * size : (at + 1) * size] for at in range(pieces)]

        def cut_columns(array, pieces):
            size = array.shape[1] // pieces
            return [array[:, at * size : (at + 1) * size] for at in range(pieces)]

        pieces = OWN * Y
        for layer in reversed(range(LAYERS)):
            qkv_full, out_full, up_full, down_full = weights[layer]
            (
                before,
                first_norm,
                mixed,
                log_total,
                context,
                middle,
                second_norm,
                activated,
                act_slope,
            ) = saved[layer]
            gains = norm_gains[layer].astype(F32)
            down_grad = grad_rows.astype(BF16)
            down_bias_grad = jnp.sum(down_grad, 0, dtype=F32)
            down_rows = spread(down_grad)
            up_grad = (dot(down_rows, down_full, 1, 1) * act_slope.astype(F32)).astype(BF16)
            norm_grad = collect(up_grad, up_full, 1)
            grad_down = settle(cut_rows(dot(activated, down_rows, 0, 0), pieces))
            grad_up = settle(cut_columns(dot(second_norm, up_grad, 0, 0), pieces))
            up_bias_grad = jnp.sum(up_grad, 0, dtype=F32)
            added, second_gain, second_shift = norm_back(middle, gains[1], norm_grad)
            grad_rows = grad_rows + added
            attn_grad = grad_rows.astype(BF16)
            out_bias_grad = jnp.sum(attn_grad, 0, dtype=F32)
            attn_rows = spread(attn_grad)
            context_grad = dot(attn_rows, out_full, 1, 1).astype(BF16)
            grad_out = settle(cut_rows(dot(context, attn_rows, 0, 0), pieces))
            mixed_grad = attend_backward(
                *split_heads(mixed),
                slopes,
                position,
                length,
                log_total,
                context_grad.reshape(seq_len, head_here, head_dim),
            ).reshape(seq_len, -1)
            grad_qkv = dot(mixed_grad, first_norm, 0, 0).reshape(3, -1, features)
            grad_qkv = settle(cut_columns(grad_qkv, pieces))
            qkv_bias_grad = jnp.sum(mixed_grad, 0, dtype=F32)
            norm_grad = collect(mixed_grad, qkv_full, 0)
            added, first_gain, first_shift = norm_back(before, gains[0], norm_grad)
            grad_rows = grad_rows + added
            grad_qkv = (
                grad_qkv.transpose(3, 0, 2, 1)
                .reshape(features, shard_heads, head_dim, 3)
                .transpose(0, 1, 3, 2)
                .reshape(features, -1)
            )
            outputs[layer] = (
                grad_qkv.astype(F32),
                grad_out.reshape(-1, features).astype(F32),
                grad_up.transpose(1, 0, 2).reshape(features, -1).astype(F32),
                grad_down.reshape(-1, features).astype(F32),
            )
            small[layer] = jnp.stack(
                [
                    first_gain,
                    second_gain,
                    first_shift,
                    second_shift,
                    out_bias_grad,
                    down_bias_grad,
                ]
            )
            bias_grads[layer] = (qkv_bias_grad.reshape(3, pieces, -1), up_bias_grad)

        bias_pieces = []
        for at in range(pieces):
            row = [bias_grads[layer][0][:, at].reshape(-1) for layer in range(LAYERS)]
            row += [
                bias_grads[layer][1].reshape(pieces, -1)[at] for layer in range(LAYERS)
            ]
            bias_pieces.append(jnp.concatenate(row)[None])
        bias_total = settle(bias_pieces, F32)[:, 0]
        grad_qkv_bias = (
            bias_total[:, :bias_cut]
            .reshape(Y, LAYERS, 3, part_width)
            .transpose(1, 2, 0, 3)
            .reshape(LAYERS, 3, shard_heads, head_dim)
            .transpose(0, 2, 1, 3)
            .reshape(LAYERS, -1)
        )
        grad_up_bias = (
            bias_total[:, bias_cut:].reshape(Y, LAYERS, -1).transpose(1, 0, 2).reshape(LAYERS, -1)
        )

        total = jnp.concatenate(small)
        for size, at in ((C, 3), (X, 1), (Y, 0), (Z, 2)):
            step = 1
            while step < size:
                def flip(*place):
                    place = list(place)
                    place[at] ^= step
                    return tuple(place)

                total = total + send(total, flip)
                step *= 2
        total = total.reshape(LAYERS, 3, 2, features)

        home = (grad_rows * keep_rows).astype(BF16).reshape(blocks, held_len, features)
        input_grad = jnp.zeros((seq_total, held_len, features), BF16)
        at_home = []
        for step in range(Y):
            outgoing = lax.dynamic_index_in_dim(
                home, jnp.clip((y_at + step) % Y - c_at * blocks, 0, blocks - 1), 0, keepdims=False
            )
            if step:
                outgoing = send(
                    outgoing,
                    lambda y, x, z, c: (
                        ((y + step) % Y, x, z, c) if (y + step) % Y // blocks == c else None
                    ),
                )
            at_home.append(outgoing)
        holder = y_at // blocks == c_at
        for step in range(Y):
            mine = at_home[step]
            shared = send(mine, lambda y, x, z, c: ((y, x, z, 1 - c) if y // blocks == c else None))
            mine = jnp.where(holder, mine, shared)
            source_y = (y_at - step) % Y
            half = held_len // C
            half_mine = lax.dynamic_slice_in_dim(mine, c_at * half, half, 0)
            for hop in range(Z):
                source_z = (z_at - hop) % Z
                if hop:
                    part = send(half_mine, lambda y, x, z, c: (y, x, (z + hop) % Z, c))
                    other = send(part, lambda y, x, z, c: (y, x, z, 1 - c))
                    block = jnp.where(
                        c_at == 0,
                        jnp.concatenate([part, other]),
                        jnp.concatenate([other, part]),
                    )
                else:
                    block = mine
                input_grad = lax.dynamic_update_index_in_dim(
                    input_grad, block, seq_deal[source_y * Z + source_z], 0
                )
        return (
            activations,
            input_grad,
            total[:, 0],
            total[:, 1],
            jnp.stack([outputs[layer][0] for layer in range(LAYERS)]),
            grad_qkv_bias,
            jnp.stack([outputs[layer][1] for layer in range(LAYERS)]),
            total[:, 2],
            jnp.stack([outputs[layer][2] for layer in range(LAYERS)]),
            grad_up_bias,
            jnp.stack([outputs[layer][3] for layer in range(LAYERS)]),
        )

    return body


def solution(mesh):
    placed = (
        P(None, "dp", None),
        P(None, "dp", None),
        P(),
        P(),
        P(),
        P(),
        P(None, None, "tensor"),
        P(None, "tensor"),
        P(None, "tensor", None),
        P(),
        P(None, None, "tensor"),
        P(None, "tensor"),
        P(None, "tensor", None),
    )
    return jax.shard_map(
        make_body(mesh.shape["dp"], mesh.shape["tensor"]),
        mesh=mesh,
        in_specs=placed,
        out_specs=(
            P("dp", None, "tensor", None),
            P(None, "dp", None),
            P(),
            P(),
            P(None, None, "tensor"),
            P(None, "tensor"),
            P(None, "tensor", None),
            P(),
            P(None, None, "tensor"),
            P(None, "tensor"),
            P(None, "tensor", None),
        ),
        check_vma=False,
    )
```

time: 1330 us -> 1000 us (0.75)
  waiting for transfers between devices: 823 us -> 350 us
  starting transfers between devices: 20.3 us -> 229 us
  blocking collectives: 68.5 us -> 0 us
  other arithmetic: 123 us -> 150 us
  matrix products: 202 us -> 179 us
    reduce_scatter x8 -> x0, waiting for transfers between devices: 350 us -> none  [the longest x4 193 us: collect(): lax.psum_scatter(fourfold.astype(jnp.bfloat16), 'tensor', scatter_dimensi...]
    ppermute x0 -> x165, waiting for transfers between devices: none -> 350 us  [send(): return lax.ppermute(value, ('dp', 'tensor'), pairs)]
    all_gather x9 -> x0, waiting for transfers between devices: 348 us -> none  [the longest x4 175 us: spread_back(): lax.all_gather(fourfold, 'tensor', axis=2, tiled=True)]
    ppermute x0 -> x165, starting transfers between devices: none -> 229 us  [send(): return lax.ppermute(value, ('dp', 'tensor'), pairs)]
    psum x1 -> x0, waiting for transfers between devices: 111 us -> none  [body(): lax.psum(stacked[0].astype(jnp.bfloat16), 'dp').astype(jnp.float32)]
    psum x2 -> x0, blocking collectives: 52.2 us -> none  [the longest x1 43 us: body(): lax.psum((norm_stacked[0], norm_stacked[1], norm_stacked[2]), ('dp', 'ten...]
    dot_general x52 -> x44, matrix products: 202 us -> 179 us  [the longest x32 97 us: dot(): lax.dot_general(left_side, right_side, (((left_dim,), (right_dim,)), ((),...]
    slice x3 -> x51, local copies, waits for them, and re-layouts: 1.22 us -> 20.1 us  [the longest x16 5.04 us: collect(): got = send(part[rows_here:], lambda y, x, z, c: (y, x, z, (c + 1) % C))]
  transfers between devices with their start and end apart: 20 -> 165, of which waited for: 19 -> 57; matrix products, arithmetic and copies ran while one was open for 5% -> 35% of each run, Pallas kernels for 0% -> 0%
where the time goes in v1:
time: 1000 us; the launch traced here: 995 us
  waiting for transfers between devices  350 us (35%)
  starting transfers between devices  229 us (23%)
  matrix products  179 us (18%)
  other arithmetic  150 us (15%)
  local copies, waits for them, and re-layouts  63.3 us (6%)
  between operations  24.6 us (2%)
    ppermute x165, waiting for transfers between devices, send(): return lax.ppermute(value, ('dp', 'tensor'), pairs)  350 us
    ppermute x165, starting transfers between devices, send(): return lax.ppermute(value, ('dp', 'tensor'), pairs)  229 us
    dot_general x32, matrix products, dot(): lax.dot_general(left_side, right_side, (((left_dim,), (right_dim,)), ((),...  97 us
    convert_element_type x16, other arithmetic, settle(): low = here.astype(wire)  22.6 us
    dot_general x2, matrix products, attend_backward(): jnp.einsum('qhd,khd->hqk', context_grad, values, preferred_element_type=F32)  22.3 us
  transfers between devices with their start and end apart: 165, of which 57 were waited for; matrix products, arithmetic and copies ran while one was open for 35% of the time, Pallas kernels for 0%

profile of v1, /device:TPU:0, one launch (start us, length us, event | category | flops | bytes accessed | tf_op | source)
XLA Modules:
  0.0 995.5 jit_solution(11676310071413778814)
XLA Ops:
  91.2 8.7 fusion.151
  100.0 8.0 exponential_reduce_fusion.1
  108.6 8.5 fusion.26
  129.8 8.8 collective-permute-done.17
  169.1 7.2 multiply_convert_fusion.5
  180.2 9.8 collective-permute-done.29
  254.0 8.8 fusion.152
  262.8 8.0 exponential_reduce_fusion
  270.8 8.5 fusion.29
  297.7 22.9 %collective-permute-start.52 = (bf16[1024,256]{0,1:T(8,128)(2,1)}, bf16[1024,256]{0,1:T(8,128)(2,1)}, u32[]{:S(2)}, u32[]{:S(2)}) collective-permute-start(bf16[1024,256]{0,1:T(8,128)(2,1)} %broadcast_select_fusion.7), channel_id=1, source_target_pairs={{0,2},{1,3},{2,0},{3,1},{4,6},{5,7},{6,4},{7,5},{8,10},{9,11},{10,... | collective-permute-start | bytes 1572872 | tf_op jit(solution)/shard_map/ppermute | solution.py:116
  345.4 7.3 collective-permute-done.56
  367.6 9.3 collective-permute-done.57
  399.0 8.3 collective-permute-done.160
  413.5 18.0 %collective-permute-done.148 = bf16[1024,256]{0,1:T(8,128)(2,1)S(1)} collective-permute-done((bf16[1024,256]{0,1:T(8,128)(2,1)S(1)}, bf16[1024,256]{0,1:T(8,128)(2,1)S(1)}, u32[]{:S(2)}, u32[]{:S(2)}) %collective-permute-start.148) | collective-permute-done | bytes 524320 | tf_op jit(solution)/shard_map/ppermute | solution.py:116
  461.3 11.3 %collective-permute-done.61 = bf16[256,1024]{1,0:T(8,128)(2,1)S(1)} collective-permute-done((bf16[256,1024]{1,0:T(8,128)(2,1)S(1)}, bf16[256,1024]{1,0:T(8,128)(2,1)S(1)}, u32[]{:S(2)}, u32[]{:S(2)}) %collective-permute-start.61) | collective-permute-done | bytes 524320 | tf_op jit(solution)/shard_map/ppermute | solution.py:116
  476.2 17.9 %collective-permute-done.162 = bf16[256,1024]{1,0:T(8,128)(2,1)} collective-permute-done((bf16[256,1024]{1,0:T(8,128)(2,1)}, bf16[256,1024]{1,0:T(8,128)(2,1)}, u32[]{:S(2)}, u32[]{:S(2)}) %collective-permute-start.162) | collective-permute-done | bytes 524320 | tf_op jit(solution)/shard_map/ppermute | solution.py:116
  515.9 13.6 %multiply_reduce_fusion.1 = (f32[4,1024]{1,0:T(4,128)S(1)}, f32[4,1024,1024]{1,2,0:T(8,128)}) fusion(f32[4,1024,1024]{1,2,0:T(8,128)} %get-tuple-element.152, f32[4,1024]{1,0:T(4,128)S(1)} %log_add_fusion, bf16[1024,4,64]{0,2,1:T(8,128)(2,1)S(1)} %bitcast.339, bf16[1024,3,4,64]{0,3,2,1:T(8,128)(2,1)} %bitcast.336), kind=kOutput, calls=%fused_computation.9 | convolution fusion | flops 549449728 | bytes 34635776 | tf_op jit(solution)/shard_map/qhd,khd->hqk/dot_general | solution.py:79
  542.0 7.9 multiply_convert_fusion.1
  607.8 13.1 %collective-permute-done.120 = bf16[3,64,1024]{2,1,0:T(8,128)(2,1)S(1)} collective-permute-done((bf16[3,64,1024]{2,1,0:T(8,128)(2,1)S(1)}, bf16[3,64,1024]{2,1,0:T(8,128)(2,1)S(1)}, u32[]{:S(2)}, u32[]{:S(2)}) %collective-permute-start.120) | collective-permute-done | bytes 393248 | tf_op jit(solution)/shard_map/ppermute | solution.py:116
  624.9 7.1 collective-permute-done.121
  633.1 7.3 collective-permute-done.80
  643.9 7.8 convert_reduce_fusion.1
  670.8 17.0 %collective-permute-done.142 = bf16[1024,256]{0,1:T(8,128)(2,1)S(1)} collective-permute-done((bf16[1024,256]{0,1:T(8,128)(2,1)S(1)}, bf16[1024,256]{0,1:T(8,128)(2,1)S(1)}, u32[]{:S(2)}, u32[]{:S(2)}) %collective-permute-start.142) | collective-permute-done | bytes 524320 | tf_op jit(solution)/shard_map/ppermute | solution.py:116
  690.6 19.3 %collective-permute-done.154 = bf16[256,1024]{1,0:T(8,128)(2,1)S(1)} collective-permute-done((bf16[256,1024]{1,0:T(8,128)(2,1)S(1)}, bf16[256,1024]{1,0:T(8,128)(2,1)S(1)}, u32[]{:S(2)}, u32[]{:S(2)}) %collective-permute-start.154) | collective-permute-done | bytes 524320 | tf_op jit(solution)/shard_map/ppermute | solution.py:116
  727.7 14.7 %collective-permute-done.155 = bf16[256,1024]{1,0:T(8,128)(2,1)} collective-permute-done((bf16[256,1024]{1,0:T(8,128)(2,1)}, bf16[256,1024]{1,0:T(8,128)(2,1)}, u32[]{:S(2)}, u32[]{:S(2)}) %collective-permute-start.155) | collective-permute-done | bytes 524320 | tf_op jit(solution)/shard_map/ppermute | solution.py:116
  746.6 19.6 %collective-permute-done.144 = bf16[1024,256]{0,1:T(8,128)(2,1)} collective-permute-done((bf16[1024,256]{0,1:T(8,128)(2,1)}, bf16[1024,256]{0,1:T(8,128)(2,1)}, u32[]{:S(2)}, u32[]{:S(2)}) %collective-permute-start.144) | collective-permute-done | bytes 524320 | tf_op jit(solution)/shard_map/ppermute | solution.py:116
  781.4 9.4 fusion.16
  790.8 8.6 multiply_reduce_fusion
  805.6 7.9 multiply_convert_fusion
  858.1 8.4 collective-permute-done.132
  943.5 11.0 %collective-permute-done.94 = bf16[128,1024]{1,0:T(8,128)(2,1)} collective-permute-done((bf16[128,1024]{1,0:T(8,128)(2,1)}, bf16[128,1024]{1,0:T(8,128)(2,1)}, u32[]{:S(2)}, u32[]{:S(2)}) %collective-permute-start.94) | collective-permute-done | bytes 262176 | tf_op jit(solution)/shard_map/ppermute | solution.py:116
  978.2 11.2 %collective-permute-done.102 = bf16[128,1024]{1,0:T(8,128)(2,1)S(1)} collective-permute-done((bf16[128,1024]{1,0:T(8,128)(2,1)}, bf16[128,1024]{1,0:T(8,128)(2,1)S(1)}, u32[]{:S(2)}, u32[]{:S(2)}) %collective-permute-start.102) | collective-permute-done | bytes 262176 | tf_op jit(solution)/shard_map/ppermute | solution.py:116
  (896 shorter events, 615.7 us)
Async XLA Ops:
  3.5 42.4 %collective-permute-start.8 = (bf16[1,896]{1,0:T(2,128)(2,1)}, bf16[1,896]{1,0:T(2,128)(2,1)}, u32[]{:S(2)}, u32[]{:S(2)}) collective-permute-start(bf16[1,896]{1,0:T(2,128)(2,1)} %constant_dynamic-update-slice_fusion), channel_id=1, source_target_pairs={{0,4},{1,5},{2,6},{3,7},{12,8},{13,9},{14,10},{15,11},{16,20},{17,... | collective-permute-start | bytes 5384 | tf_op jit(solution)/shard_map/ppermute | solution.py:116
  13.2 52.2 %collective-permute-start.12 = (bf16[64,1024]{1,0:T(8,128)(2,1)}, bf16[64,1024]{1,0:T(8,128)(2,1)S(1)}, u32[]{:S(2)}, u32[]{:S(2)}) collective-permute-start(bf16[64,1024]{1,0:T(8,128)(2,1)} %dynamic-slice_bitcast_fusion.10), channel_id=1, source_target_pairs={{0,4},{1,5},{2,6},{3,7},{12,8},{13,9},{14,10},{15,11},{16,20},{17,... | collective-permute-start | bytes 393224 | tf_op jit(solution)/shard_map/ppermute | solution.py:116
  66.0 63.8 %collective-permute-start.66 = (bf16[256,1024]{1,0:T(8,128)(2,1)}, bf16[256,1024]{1,0:T(8,128)(2,1)S(1)}, u32[]{:S(2)}, u32[]{:S(2)}) collective-permute-start(bf16[256,1024]{1,0:T(8,128)(2,1)} %dynamic-slice_bitcast_fusion), channel_id=1, source_target_pairs={{0,16},{2,18},{4,20},{6,22},{8,24},{10,26},{12,28},{14,30},{17,1},... | collective-permute-start | bytes 1572872 | tf_op jit(solution)/shard_map/ppermute | solution.py:116
  68.1 57.2 %collective-permute-start.22 = (bf16[1024,256]{0,1:T(8,128)(2,1)}, bf16[1024,256]{0,1:T(8,128)(2,1)}, u32[]{:S(2)}, u32[]{:S(2)}) collective-permute-start(bf16[1024,256]{0,1:T(8,128)(2,1)} %bitcast.24), channel_id=1, source_target_pairs={{0,4},{1,5},{2,6},{3,7},{12,8},{13,9},{14,10},{15,11},{16,20},{17,... | collective-permute-start | bytes 1572872 | tf_op jit(solution)/shard_map/ppermute | solution.py:116
  239.9 40.3 %collective-permute-start.41 = (bf16[64,1024]{1,0:T(8,128)(2,1)}, bf16[64,1024]{1,0:T(8,128)(2,1)}, u32[]{:S(2)}, u32[]{:S(2)}) collective-permute-start(bf16[64,1024]{1,0:T(8,128)(2,1)} %broadcast_select_fusion.17), channel_id=1, source_target_pairs={{0,16},{1,17},{2,18},{3,19},{4,20},{5,21},{6,22},{7,23},{8,24},{9,... | collective-permute-start | bytes 393224 | tf_op jit(solution)/shard_map/ppermute | solution.py:116
  240.7 39.4 %collective-permute-start.43 = (bf16[64,1024]{1,0:T(8,128)(2,1)}, bf16[64,1024]{1,0:T(8,128)(2,1)}, u32[]{:S(2)}, u32[]{:S(2)}) collective-permute-start(bf16[64,1024]{1,0:T(8,128)(2,1)} %collective-permute-done.42), channel_id=1, source_target_pairs={{0,16},{1,17},{2,18},{3,19},{4,20},{5,21},{6,22},{7,23},{8,24},{9,... | collective-permute-start | bytes 393224 | tf_op jit(solution)/shard_map/ppermute | solution.py:116
  288.7 50.9 %collective-permute-start.54 = (bf16[256,1024]{1,0:T(8,128)(2,1)}, bf16[256,1024]{1,0:T(8,128)(2,1)}, u32[]{:S(2)}, u32[]{:S(2)}) collective-permute-start(bf16[256,1024]{1,0:T(8,128)(2,1)} %dynamic-slice_bitcast_fusion.1), channel_id=1, source_target_pairs={{0,4},{1,5},{2,6},{3,7},{12,8},{13,9},{14,10},{15,11},{16,20},{17,... | collective-permute-start | bytes 1572872 | tf_op jit(solution)/shard_map/ppermute | solution.py:116
  297.7 44.3 %collective-permute-start.52 = (bf16[1024,256]{0,1:T(8,128)(2,1)}, bf16[1024,256]{0,1:T(8,128)(2,1)}, u32[]{:S(2)}, u32[]{:S(2)}) collective-permute-start(bf16[1024,256]{0,1:T(8,128)(2,1)} %broadcast_select_fusion.7), channel_id=1, source_target_pairs={{0,2},{1,3},{2,0},{3,1},{4,6},{5,7},{6,4},{7,5},{8,10},{9,11},{10,... | collective-permute-start | bytes 1572872 | tf_op jit(solution)/shard_map/ppermute | solution.py:116
  386.7 46.0 %collective-permute-start.72 = (bf16[256,1024]{1,0:T(8,128)(2,1)S(1)}, bf16[256,1024]{1,0:T(8,128)(2,1)S(1)}, u32[]{:S(2)}, u32[]{:S(2)}) collective-permute-start(bf16[256,1024]{1,0:T(8,128)(2,1)S(1)} %slice.725), channel_id=1, source_target_pairs={{0,1},{1,0},{2,3},{3,2},{4,5},{5,4},{6,7},{7,6},{8,9},{9,8},{10,11... | collective-permute-start | bytes 1572872 | tf_op jit(solution)/shard_map/ppermute | solution.py:116
  390.2 47.1 %collective-permute-start.60 = (bf16[256,1024]{1,0:T(8,128)(2,1)S(1)}, bf16[256,1024]{1,0:T(8,128)(2,1)S(1)}, u32[]{:S(2)}, u32[]{:S(2)}) collective-permute-start(bf16[256,1024]{1,0:T(8,128)(2,1)S(1)} %slice.718), channel_id=1, source_target_pairs={{0,1},{1,0},{2,3},{3,2},{4,5},{5,4},{6,7},{7,6},{8,9},{9,8},{10,11... | collective-permute-start | bytes 1572872 | tf_op jit(solution)/shard_map/ppermute | solution.py:116
  407.3 44.5 %collective-permute-start.159 = (bf16[256,1024]{1,0:T(8,128)(2,1)S(1)}, bf16[256,1024]{1,0:T(8,128)(2,1)S(1)}, u32[]{:S(2)}, u32[]{:S(2)}) collective-permute-start(bf16[256,1024]{1,0:T(8,128)(2,1)S(1)} %get-tuple-element.64), channel_id=1, source_target_pairs={{0,16},{1,17},{2,18},{3,19},{4,20},{5,21},{6,22},{7,23},{8,24},{9,... | collective-permute-start | bytes 1572872 | tf_op jit(solution)/shard_map/ppermute | solution.py:116
  450.0 48.0 %collective-permute-start.74 = (bf16[256,1024]{1,0:T(8,128)(2,1)}, bf16[256,1024]{1,0:T(8,128)(2,1)}, u32[]{:S(2)}, u32[]{:S(2)}) collective-permute-start(bf16[256,1024]{1,0:T(8,128)(2,1)} %get-tuple-element.42), channel_id=1, source_target_pairs={{0,8},{1,9},{2,10},{3,11},{4,12},{5,13},{6,14},{7,15},{8,0},{9,1},... | collective-permute-start | bytes 1572872 | tf_op jit(solution)/shard_map/ppermute | solution.py:116
  451.8 61.5 %collective-permute-start.73 = (bf16[256,1024]{1,0:T(8,128)(2,1)}, bf16[256,1024]{1,0:T(8,128)(2,1)}, u32[]{:S(2)}, u32[]{:S(2)}) collective-permute-start(bf16[256,1024]{1,0:T(8,128)(2,1)} %get-tuple-element.42), channel_id=1, source_target_pairs={{0,1},{1,0},{2,3},{3,2},{4,5},{5,4},{6,7},{7,6},{8,9},{9,8},{10,11... | collective-permute-start | bytes 1572872 | tf_op jit(solution)/shard_map/ppermute | solution.py:116
  454.2 39.9 %collective-permute-start.162 = (bf16[256,1024]{1,0:T(8,128)(2,1)}, bf16[256,1024]{1,0:T(8,128)(2,1)}, u32[]{:S(2)}, u32[]{:S(2)}) collective-permute-start(bf16[256,1024]{1,0:T(8,128)(2,1)} %fusion.76), channel_id=1, source_target_pairs={{4,0},{5,1},{6,2},{7,3},{8,12},{9,13},{10,14},{11,15},{20,16},{21,... | collective-permute-start | bytes 1572872 | tf_op jit(solution)/shard_map/ppermute | solution.py:116
  460.1 45.2 %collective-permute-start.150 = (bf16[1024,256]{0,1:T(8,128)(2,1)}, bf16[1024,256]{0,1:T(8,128)(2,1)}, u32[]{:S(2)}, u32[]{:S(2)}) collective-permute-start(bf16[1024,256]{0,1:T(8,128)(2,1)} %fusion.74), channel_id=1, source_target_pairs={{4,0},{5,1},{6,2},{7,3},{8,12},{9,13},{10,14},{11,15},{20,16},{21,... | collective-permute-start | bytes 1572872 | tf_op jit(solution)/shard_map/ppermute | solution.py:116
  507.0 49.2 %collective-permute-start.163 = (bf16[256,1024]{1,0:T(8,128)(2,1)}, bf16[256,1024]{1,0:T(8,128)(2,1)}, u32[]{:S(2)}, u32[]{:S(2)}) collective-permute-start(bf16[256,1024]{1,0:T(8,128)(2,1)} %add_convert_fusion.4), channel_id=1, source_target_pairs={{0,8},{1,9},{2,10},{3,11},{12,4},{13,5},{14,6},{15,7},{16,24},{17,... | collective-permute-start | bytes 1572872 | tf_op jit(solution)/shard_map/ppermute | solution.py:116
  509.1 61.2 %collective-permute-start.151 = (bf16[1024,256]{0,1:T(8,128)(2,1)S(1)}, bf16[1024,256]{0,1:T(8,128)(2,1)}, u32[]{:S(2)}, u32[]{:S(2)}) collective-permute-start(bf16[1024,256]{0,1:T(8,128)(2,1)S(1)} %add_convert_fusion.6), channel_id=1, source_target_pairs={{0,8},{1,9},{2,10},{3,11},{12,4},{13,5},{14,6},{15,7},{16,24},{17,... | collective-permute-start | bytes 1572872 | tf_op jit(solution)/shard_map/ppermute | solution.py:116
  557.5 38.7 %collective-permute-start.164 = (bf16[256,1024]{1,0:T(8,128)(2,1)S(1)}, bf16[256,1024]{1,0:T(8,128)(2,1)}, u32[]{:S(2)}, u32[]{:S(2)}) collective-permute-start(bf16[256,1024]{1,0:T(8,128)(2,1)S(1)} %broadcast_select_fusion.1), channel_id=1, source_target_pairs={{0,16},{1,17},{2,18},{3,19},{4,20},{5,21},{6,22},{7,23},{8,24},{9,... | collective-permute-start | bytes 1572872 | tf_op jit(solution)/shard_map/ppermute | solution.py:116
  599.9 42.1 %collective-permute-start.140 = (bf16[64,1024]{1,0:T(8,128)(2,1)S(1)}, bf16[64,1024]{1,0:T(8,128)(2,1)S(1)}, u32[]{:S(2)}, u32[]{:S(2)}) collective-permute-start(bf16[64,1024]{1,0:T(8,128)(2,1)S(1)} %broadcast_select_fusion.15), channel_id=1, source_target_pairs={{0,16},{1,17},{2,18},{3,19},{4,20},{5,21},{6,22},{7,23},{8,24},{9,... | collective-permute-start | bytes 393224 | tf_op jit(solution)/shard_map/ppermute | solution.py:116
  657.4 54.1 %collective-permute-start.84 = (bf16[256,1024]{1,0:T(8,128)(2,1)S(1)}, bf16[256,1024]{1,0:T(8,128)(2,1)S(1)}, u32[]{:S(2)}, u32[]{:S(2)}) collective-permute-start(bf16[256,1024]{1,0:T(8,128)(2,1)S(1)} %slice.737), channel_id=1, source_target_pairs={{0,1},{1,0},{2,3},{3,2},{4,5},{5,4},{6,7},{7,6},{8,9},{9,8},{10,11... | collective-permute-start | bytes 1572872 | tf_op jit(solution)/shard_map/ppermute | solution.py:116
  661.8 57.3 %collective-permute-start.141 = (bf16[1024,256]{0,1:T(8,128)(2,1)S(1)}, bf16[1024,256]{0,1:T(8,128)(2,1)S(1)}, u32[]{:S(2)}, u32[]{:S(2)}) collective-permute-start(bf16[1024,256]{0,1:T(8,128)(2,1)S(1)} %get-tuple-element.66), channel_id=1, source_target_pairs={{0,16},{1,17},{2,18},{3,19},{4,20},{5,21},{6,22},{7,23},{8,24},{9,... | collective-permute-start | bytes 1572872 | tf_op jit(solution)/shard_map/ppermute | solution.py:116
  668.6 59.1 %collective-permute-start.153 = (bf16[256,1024]{1,0:T(8,128)(2,1)}, bf16[256,1024]{1,0:T(8,128)(2,1)}, u32[]{:S(2)}, u32[]{:S(2)}) collective-permute-start(bf16[256,1024]{1,0:T(8,128)(2,1)} %get-tuple-element.62), channel_id=1, source_target_pairs={{0,16},{1,17},{2,18},{3,19},{4,20},{5,21},{6,22},{7,23},{8,24},{9,... | collective-permute-start | bytes 1572872 | tf_op jit(solution)/shard_map/ppermute | solution.py:116
  669.5 40.4 %collective-permute-start.154 = (bf16[256,1024]{1,0:T(8,128)(2,1)S(1)}, bf16[256,1024]{1,0:T(8,128)(2,1)S(1)}, u32[]{:S(2)}, u32[]{:S(2)}) collective-permute-start(bf16[256,1024]{1,0:T(8,128)(2,1)S(1)} %get-tuple-element.63), channel_id=1, source_target_pairs={{0,16},{1,17},{2,18},{3,19},{4,20},{5,21},{6,22},{7,23},{8,24},{9,... | collective-permute-start | bytes 1572872 | tf_op jit(solution)/shard_map/ppermute | solution.py:116
  725.8 40.4 %collective-permute-start.144 = (bf16[1024,256]{0,1:T(8,128)(2,1)}, bf16[1024,256]{0,1:T(8,128)(2,1)}, u32[]{:S(2)}, u32[]{:S(2)}) collective-permute-start(bf16[1024,256]{0,1:T(8,128)(2,1)} %fusion.73), channel_id=1, source_target_pairs={{4,0},{5,1},{6,2},{7,3},{8,12},{9,13},{10,14},{11,15},{20,16},{21,... | collective-permute-start | bytes 1572872 | tf_op jit(solution)/shard_map/ppermute | solution.py:116
  769.0 50.8 %collective-permute-start.145 = (bf16[1024,256]{0,1:T(8,128)(2,1)}, bf16[1024,256]{0,1:T(8,128)(2,1)}, u32[]{:S(2)}, u32[]{:S(2)}) collective-permute-start(bf16[1024,256]{0,1:T(8,128)(2,1)} %add_convert_fusion.7), channel_id=1, source_target_pairs={{0,8},{1,9},{2,10},{3,11},{12,4},{13,5},{14,6},{15,7},{16,24},{17,... | collective-permute-start | bytes 1572872 | tf_op jit(solution)/shard_map/ppermute | solution.py:116
  776.6 50.8 %collective-permute-start.157 = (bf16[256,1024]{1,0:T(8,128)(2,1)}, bf16[256,1024]{1,0:T(8,128)(2,1)}, u32[]{:S(2)}, u32[]{:S(2)}) collective-permute-start(bf16[256,1024]{1,0:T(8,128)(2,1)} %add_convert_fusion.5), channel_id=1, source_target_pairs={{0,8},{1,9},{2,10},{3,11},{12,4},{13,5},{14,6},{15,7},{16,24},{17,... | collective-permute-start | bytes 1572872 | tf_op jit(solution)/shard_map/ppermute | solution.py:116
  803.5 50.5 %collective-permute-start.129 = (bf16[64,1024]{1,0:T(8,128)(2,1)}, bf16[64,1024]{1,0:T(8,128)(2,1)S(1)}, u32[]{:S(2)}, u32[]{:S(2)}) collective-permute-start(bf16[64,1024]{1,0:T(8,128)(2,1)} %get-tuple-element.89), channel_id=1, source_target_pairs={{0,16},{1,17},{2,18},{3,19},{4,20},{5,21},{6,22},{7,23},{8,24},{9,... | collective-permute-start | bytes 393224 | tf_op jit(solution)/shard_map/ppermute | solution.py:116
  804.4 44.9 %collective-permute-start.130 = (bf16[64,1024]{1,0:T(8,128)(2,1)}, bf16[64,1024]{1,0:T(8,128)(2,1)}, u32[]{:S(2)}, u32[]{:S(2)}) collective-permute-start(bf16[64,1024]{1,0:T(8,128)(2,1)} %get-tuple-element.90), channel_id=1, source_target_pairs={{0,16},{1,17},{2,18},{3,19},{4,20},{5,21},{6,22},{7,23},{8,24},{9,... | collective-permute-start | bytes 393224 | tf_op jit(solution)/shard_map/ppermute | solution.py:116
  821.8 49.6 %collective-permute-start.146 = (bf16[1024,256]{0,1:T(8,128)(2,1)}, bf16[1024,256]{0,1:T(8,128)(2,1)}, u32[]{:S(2)}, u32[]{:S(2)}) collective-permute-start(bf16[1024,256]{0,1:T(8,128)(2,1)} %broadcast_select_fusion.6), channel_id=1, source_target_pairs={{0,16},{1,17},{2,18},{3,19},{4,20},{5,21},{6,22},{7,23},{8,24},{9,... | collective-permute-start | bytes 1572872 | tf_op jit(solution)/shard_map/ppermute | solution.py:116
  836.4 45.2 %collective-permute-start.158 = (bf16[256,1024]{1,0:T(8,128)(2,1)}, bf16[256,1024]{1,0:T(8,128)(2,1)}, u32[]{:S(2)}, u32[]{:S(2)}) collective-permute-start(bf16[256,1024]{1,0:T(8,128)(2,1)} %broadcast_select_fusion.2), channel_id=1, source_target_pairs={{0,16},{1,17},{2,18},{3,19},{4,20},{5,21},{6,22},{7,23},{8,24},{9,... | collective-permute-start | bytes 1572872 | tf_op jit(solution)/shard_map/ppermute | solution.py:116
  853.8 37.7 %collective-permute-start.90 = (bf16[256,1024]{1,0:T(8,128)(2,1)}, bf16[256,1024]{1,0:T(8,128)(2,1)}, u32[]{:S(2)}, u32[]{:S(2)}) collective-permute-start(bf16[256,1024]{1,0:T(8,128)(2,1)} %slice.743), channel_id=1, source_target_pairs={{0,1},{1,0},{2,3},{3,2},{4,5},{5,4},{6,7},{7,6},{8,9},{9,8},{10,11... | collective-permute-start | bytes 1572872 | tf_op jit(solution)/shard_map/ppermute | solution.py:116
  879.1 49.8 %collective-permute-start.134 = (bf16[64,1024]{1,0:T(8,128)(2,1)S(1)}, bf16[64,1024]{1,0:T(8,128)(2,1)}, u32[]{:S(2)}, u32[]{:S(2)}) collective-permute-start(bf16[64,1024]{1,0:T(8,128)(2,1)S(1)} %broadcast_select_fusion.16), channel_id=1, source_target_pairs={{0,16},{1,17},{2,18},{3,19},{4,20},{5,21},{6,22},{7,23},{8,24},{9,... | collective-permute-start | bytes 393224 | tf_op jit(solution)/shard_map/ppermute | solution.py:116
  (269 other events, 5230.2 us)

commit v2 on v1

--- a/solution.py
+++ b/solution.py
@@ -1,8 +1,12 @@
+import functools
 import math
 
 import jax
 import jax.numpy as jnp
 from jax import lax
+from jax.experimental import pallas as pl
+from jax.experimental.pallas import tpu as pltpu
+from jax.sharding import Mesh
 from jax.sharding import PartitionSpec as P
 
 HEADS = 16
@@ -10,6 +14,7 @@
 EPSILON = 1e-05
 BF16 = jnp.bfloat16
 F32 = jnp.float32
+BIAS_ROWS = 8
 
 
 def dot(left_side, right_side, left_dim, right_dim):
@@ -55,40 +60,131 @@
     return values * half, slope
 
 
-def score_table(queries, key_rows, slopes, position, length):
-    scaling = queries.shape[2] ** (-0.5)
-    scores = jnp.einsum("qhd,khd->hqk", queries, key_rows, preferred_element_type=F32) * scaling
-    offset = (position[None, :] - position[:, None]).astype(F32)
-    scores = scores + slopes[:, None, None] * offset
-    allowed = (position[None, :] <= position[:, None]) & (position[None, :] < length)
-    return jnp.where(allowed[None], scores, -1e30)
-
-
-def attend_forward(queries, key_rows, values, slopes, position, length):
-    scores = score_table(queries, key_rows, slopes, position, length)
-    highest = jnp.max(scores, -1, keepdims=True)
-    log_total = highest + jnp.log(jnp.sum(jnp.exp(scores - highest), -1, keepdims=True))
-    weights = jnp.exp(scores - log_total).astype(BF16)
-    context = jnp.einsum("hqk,khd->qhd", weights, values, preferred_element_type=F32)
-    return context.astype(BF16), log_total
-
-
-def attend_backward(queries, key_rows, values, slopes, position, length, log_total, context_grad):
-    scaling = queries.shape[2] ** (-0.5)
-    weights = jnp.exp(score_table(queries, key_rows, slopes, position, length) - log_total)
-    weight_grad = jnp.einsum("qhd,khd->hqk", context_grad, values, preferred_element_type=F32)
-    value_grad = jnp.einsum(
-        "hqk,qhd->khd", weights.astype(BF16), context_grad, preferred_element_type=F32
-    )
-    center = jnp.sum(weight_grad * weights, -1, keepdims=True)
-    score_grad = (weights * (weight_grad - center)).astype(BF16)
-    query_grad = (
-        jnp.einsum("hqk,khd->qhd", score_grad, key_rows, preferred_element_type=F32) * scaling
-    )
-    key_grad = (
-        jnp.einsum("hqk,qhd->khd", score_grad, queries, preferred_element_type=F32) * scaling
-    )
-    return jnp.stack([query_grad, key_grad, value_grad], 1).astype(BF16)
+LOG2E = math.log2(math.e)
+
+def nt(a, b):
+    return lax.dot_general(a, b, (((1,), (1,)), ((), ())), preferred_element_type=F32)
+def nn(a, b):
+    return lax.dot_general(a, b, (((1,), (0,)), ((), ())), preferred_element_type=F32)
+def tn(a, b):
+    return lax.dot_general(a, b, (((0,), (0,)), ((), ())), preferred_element_type=F32)
+
+def forward_kernel(heads, width, block, places, length, slopes, mixed, context, totals, q_s, k_s, v_s, c_s):
+    seq_len = mixed.shape[0]
+    count = places.shape[0]
+    held = seq_len // count
+    span = heads * width
+    for at in range(count):
+        to = pl.ds(pl.multiple_of(places[at] * held, held), held)
+        rows = mixed[at * held:(at + 1) * held, :]
+        for head in range(heads):
+            q_s[head, to, :] = rows[:, head * width:(head + 1) * width]
+            k_s[head, to, :] = rows[:, span + head * width:span + (head + 1) * width]
+            v_s[head, to, :] = rows[:, 2 * span + head * width:2 * span + (head + 1) * width]
+    limit = length[0]
+    row = lax.broadcasted_iota(jnp.int32, (seq_len, 1), 0)
+    inside = (lax.broadcasted_iota(jnp.int32, (block, block), 0)
+              <= lax.broadcasted_iota(jnp.int32, (block, block), 1))
+    scale = LOG2E / math.sqrt(width)
+    for head in range(heads):
+        bias = jnp.where(row < limit, slopes[head] * LOG2E * row.astype(F32), -1e30)
+        for at in range(seq_len // block):
+            low, high = at * block, (at + 1) * block
+            scores = nt(k_s[head, :high, :], q_s[head, low:high, :]) * scale + bias[:high]
+            tail = jnp.where(inside, scores[low:], -1e30)
+            scores = jnp.concatenate([scores[:low], tail], 0) if at else tail
+            top = jnp.max(scores, 0, keepdims=True)
+            probs = jnp.exp2(scores - top)
+            total = jnp.sum(probs, 0, keepdims=True)
+            probs = (probs * (1.0 / total)).astype(BF16)
+            c_s[head, low:high, :] = tn(probs, v_s[head, :high, :]).astype(BF16)
+            totals[head:head + 1, low:high] = top + jnp.log2(total)
+    for at in range(count):
+        frm = pl.ds(pl.multiple_of(places[at] * held, held), held)
+        context[at * held:(at + 1) * held, :] = jnp.concatenate([c_s[head, frm, :] for head in range(heads)], 1)
+
+def attend_forward(mixed, places, length, slopes, heads, width):
+    seq_len = mixed.shape[0]
+    block = min(256, seq_len)
+    return pl.pallas_call(
+        functools.partial(forward_kernel, heads, width, block),
+        out_shape=[jax.ShapeDtypeStruct((seq_len, heads * width), BF16), jax.ShapeDtypeStruct((8, seq_len), F32)],
+        in_specs=[pl.BlockSpec(memory_space=pltpu.SMEM)] * 3 + [pl.BlockSpec(memory_space=pltpu.VMEM)],
+        out_specs=[pl.BlockSpec(memory_space=pltpu.VMEM)] * 2,
+        scratch_shapes=[pltpu.VMEM((heads, seq_len, width), BF16)] * 4,
+        compiler_params=pltpu.CompilerParams(vmem_limit_bytes=48 * 2**20),
+        cost_estimate=pl.CostEstimate(flops=4 * heads * seq_len * seq_len * width, bytes_accessed=3 * 2**20, transcendentals=heads * seq_len * seq_len // 2),
+    )(places, length, slopes, mixed)
+
+def backward_kernel(heads, width, block, places, length, slopes, mixed, context, context_grad, totals, mixed_grad,
+                    q_s, k_s, v_s, g_s, dq_s, dk_s, dv_s, stat_s):
+    seq_len = mixed.shape[0]
+    count = places.shape[0]
+    held = seq_len // count
+    span = heads * width
+    wide = lax.broadcasted_iota(jnp.int32, (held, 128), 1)
+    delta_s = stat_s
+    for at in range(count):
+        to = pl.ds(pl.multiple_of(places[at] * held, held), held)
+        rows = mixed[at * held:(at + 1) * held, :]
+        grads = context_grad[at * held:(at + 1) * held, :]
+        product = grads.astype(F32) * context[at * held:(at + 1) * held, :].astype(F32)
+        packed = jnp.zeros((held, 128), F32)
+        for head in range(heads):
+            q_s[head, to, :] = rows[:, head * width:(head + 1) * width]
+            k_s[head, to, :] = rows[:, span + head * width:span + (head + 1) * width]
+            v_s[head, to, :] = rows[:, 2 * span + head * width:2 * span + (head + 1) * width]
+            g_s[head, to, :] = grads[:, head * width:(head + 1) * width]
+            packed = jnp.where(wide == head, jnp.sum(product[:, head * width:(head + 1) * width], 1, keepdims=True), packed)
+        delta_s[to, :] = packed
+    limit = length[0]
+    row = lax.broadcasted_iota(jnp.int32, (seq_len, 1), 0)
+    inside = (lax.broadcasted_iota(jnp.int32, (block, block), 0)
+              <= lax.broadcasted_iota(jnp.int32, (block, block), 1))
+    scale = LOG2E / math.sqrt(width)
+    down = 1.0 / math.sqrt(width)
+    delta_rows = jnp.transpose(stat_s[...])
+    for head in range(heads):
+        bias = jnp.where(row < limit, slopes[head] * LOG2E * row.astype(F32), -1e30)
+        for at in range(seq_len // block):
+            low, high = at * block, (at + 1) * block
+            query = q_s[head, low:high, :]
+            grads = g_s[head, low:high, :]
+            keys = k_s[head, :high, :]
+            scores = nt(keys, query) * scale + bias[:high]
+            probs = jnp.exp2(scores - totals[head:head + 1, low:high])
+            tail = jnp.where(inside, probs[low:], 0.0)
+            probs = jnp.concatenate([probs[:low], tail], 0) if at else tail
+            low_probs = probs.astype(BF16)
+            dprobs = nt(v_s[head, :high, :], grads)
+            dscores = (probs * (dprobs - delta_rows[head:head + 1, low:high])).astype(BF16)
+            dv = nn(low_probs, grads)
+            dk = nn(dscores, query)
+            if at:
+                dv_s[head, :low, :] += dv[:low]
+                dk_s[head, :low, :] += dk[:low]
+            dv_s[head, low:high, :] = dv[low:]
+            dk_s[head, low:high, :] = dk[low:]
+            dq_s[head, low:high, :] = tn(dscores, keys)
+    for at in range(count):
+        frm = pl.ds(pl.multiple_of(places[at] * held, held), held)
+        mixed_grad[at * held:(at + 1) * held, :] = jnp.concatenate(
+            [(dq_s[head, frm, :] * down).astype(BF16) for head in range(heads)]
+            + [(dk_s[head, frm, :] * down).astype(BF16) for head in range(heads)]
+            + [dv_s[head, frm, :].astype(BF16) for head in range(heads)], 1)
+
+def attend_backward(mixed, context, context_grad, totals, places, length, slopes, heads, width):
+    seq_len = mixed.shape[0]
+    block = min(256, seq_len)
+    return pl.pallas_call(
+        functools.partial(backward_kernel, heads, width, block),
+        out_shape=jax.ShapeDtypeStruct(mixed.shape, BF16),
+        in_specs=[pl.BlockSpec(memory_space=pltpu.SMEM)] * 3 + [pl.BlockSpec(memory_space=pltpu.VMEM)] * 4,
+        out_specs=pl.BlockSpec(memory_space=pltpu.VMEM),
+        scratch_shapes=[pltpu.VMEM((heads, seq_len, width), BF16)] * 4 + [pltpu.VMEM((heads, seq_len, width), F32)] * 3 + [pltpu.VMEM((seq_len, 128), F32)],
+        compiler_params=pltpu.CompilerParams(vmem_limit_bytes=48 * 2**20),
+        cost_estimate=pl.CostEstimate(flops=10 * heads * seq_len * seq_len * width, bytes_accessed=6 * 2**20, transcendentals=heads * seq_len * seq_len // 2),
+    )(places, length, slopes, mixed, context, context_grad, totals)
 
 
 def make_body(data_size, tensor_size):
@@ -97,6 +193,7 @@
     C = 2
     Z = tensor_size // C
     OWN = Z // X
+    AXES = ("y", "x", "z", "c")
 
     def send(value, rule):
         pairs = []
@@ -113,7 +210,7 @@
                                     ((ty * X + tx) * Z + tz) * C + tc,
                                 )
                             )
-        return lax.ppermute(value, ("dp", "tensor"), pairs)
+        return lax.ppermute(value, AXES, pairs)
 
     def body(
         tokens,
@@ -130,10 +227,7 @@
         up_bias,
         down_weight,
     ):
-        data_rank = lax.axis_index("dp")
-        tensor_rank = lax.axis_index("tensor")
-        y_at, x_at = data_rank // X, data_rank % X
-        z_at, c_at = tensor_rank // C, tensor_rank % C
+        y_at, x_at, z_at, c_at = (lax.axis_index(name) for name in ("y", "x", "z", "c"))
         seq_total, held_len, features = tokens.shape
         head_dim = features // HEADS
         group = X * C
@@ -166,45 +260,81 @@
                 total = part if total is None else total + part
             return total
 
-        def fetch(piece):
-            arrived = None
-            for step in range(1, Z // OWN):
-                got = send(
-                    piece,
-                    lambda y, x, z, c: (
-                        (y, x, (z + OWN * step) % Z, c) if z // OWN == x else None
-                    ),
-                )
-                arrived = got if arrived is None else arrived + got
-            piece = jnp.where(is_owner, piece, arrived)
-            shards = [piece] + [
-                send(piece, lambda y, x, z, c: (y, x, z // OWN * OWN + (z - step) % OWN, c))
-                for step in range(1, OWN)
-            ]
-            full = []
-            for shard in shards:
-                full.append(shard)
-                for step in range(1, Y):
-                    full.append(send(shard, lambda y, x, z, c: ((y - step) % Y, x, z, c)))
-            return full
-
-        def settle(parts, wire=BF16):
-            sums = []
-            for shard in range(OWN):
-                here = parts[shard * Y].astype(F32)
-                for step in range(1, Y):
-                    here += send(
-                        parts[shard * Y + step].astype(wire),
-                        lambda y, x, z, c: ((y + step) % Y, x, z, c),
-                    ).astype(F32)
-                sums.append(here)
-            here = sums[0]
+        shard_heads = qkv_weight.shape[2] // (3 * head_dim)
+        shard_width = shard_heads * head_dim
+        cut_by_x = shard_heads % X == 0
+        xs = X if cut_by_x else 1
+        shards = Z if cut_by_x else OWN
+        splits = xs * Y
+        part_at = x_at * Y + y_at if cut_by_x else y_at
+
+        def own_part(array, axis):
+            size = array.shape[axis] // splits
+            return lax.dynamic_slice_in_dim(array, part_at * size, size, axis)
+
+        def fetch(bundle, cuts):
+            if cut_by_x:
+                got = lax.all_gather(bundle, "z", axis=0)
+            else:
+                arrived = None
+                for step in range(1, Z // OWN):
+                    here = send(
+                        bundle,
+                        lambda y, x, z, c: (
+                            (y, x, (z + OWN * step) % Z, c) if z // OWN == x else None
+                        ),
+                    )
+                    arrived = here if arrived is None else arrived + here
+                bundle = jnp.where(is_owner, bundle, arrived)
+                got = jnp.stack(
+                    [bundle]
+                    + [
+                        send(
+                            bundle,
+                            lambda y, x, z, c: (y, x, z // OWN * OWN + (z - step) % OWN, c),
+                        )
+                        for step in range(1, OWN)
+                    ]
+                )
+            results = []
+            at = 0
+            for cut in cuts:
+                piece = got[:, at : at + cut]
+                at += cut
+                results.append(
+                    jnp.stack(
+                        [piece]
+                        + [
+                            send(piece, lambda y, x, z, c: ((y - step) % Y, x, z, c))
+                            for step in range(1, Y)
+                        ]
+                    )
+                )
+            return results
+
+        def sum_over_y(parts):
+            here = parts[0].astype(F32)
+            for step in range(1, Y):
+                here += send(
+                    parts[step].astype(BF16), lambda y, x, z, c: ((y + step) % Y, x, z, c)
+                ).astype(F32)
+            return here.astype(BF16)
+
+        def settle(sums):
+            rows = sums.shape[1]
+            if cut_by_x:
+                low = lax.psum_scatter(
+                    sums.reshape(-1, features), "z", scatter_dimension=0, tiled=True
+                )
+                full = lax.all_gather(low, ("y", "x"), axis=0)
+                return full.reshape(Y, X, rows, features).swapaxes(0, 1).reshape(-1, rows, features)
+            here = sums[0].astype(F32)
             for step in range(1, OWN):
                 here += send(
-                    sums[step].astype(wire),
+                    sums[step],
                     lambda y, x, z, c: (y, x, z // OWN * OWN + (z + step) % OWN, c),
                 ).astype(F32)
-            low = here.astype(wire)
+            low = here.astype(BF16)
             for step in range(1, Z // OWN):
                 here += send(
                     low,
@@ -214,7 +344,7 @@
                         else None
                     ),
                 ).astype(F32)
-            low = here.astype(wire)
+            low = here.astype(BF16)
             arrived = None
             for step in range(1, X):
                 got = send(
@@ -226,34 +356,24 @@
             relative = [low] + [
                 send(low, lambda y, x, z, c: ((y - step) % Y, x, z, c)) for step in range(1, Y)
             ]
-            stacked = jnp.stack(relative)
-            return jnp.roll(stacked, y_at, 0) if Y > 2 else jnp.where(
-                y_at == 0, stacked, stacked[::-1]
-            )
-
-        def own_part(array, axis):
-            size = array.shape[axis] // Y
-            return lax.dynamic_slice_in_dim(array, y_at * size, size, axis)
-
-        shard_heads = qkv_weight.shape[2] // (3 * head_dim)
-        shard_width = shard_heads * head_dim
-        weights = []
-        bias_rows = []
-        qkv_bias_view = (
+            return jnp.roll(jnp.stack(relative), y_at, 0)
+
+        part_width = shard_width // splits
+        hidden_part = down_weight.shape[1] // splits
+        qkv_bias_part = own_part(
             qkv_bias.reshape(LAYERS, shard_heads, 3, head_dim)
             .transpose(0, 2, 1, 3)
-            .reshape(LAYERS, 3, shard_width)
-        )
-        qkv_bias_part = own_part(qkv_bias_view, 2).reshape(1, -1)
-        up_bias_part = own_part(up_bias, 1).reshape(1, -1)
-        bias_cut = qkv_bias_part.shape[1]
-        bias_parts = fetch(jnp.concatenate([qkv_bias_part, up_bias_part], 1))
-        full_qkv_bias = jnp.concatenate(
-            [part[0, :bias_cut].reshape(LAYERS, 3, -1) for part in bias_parts], 2
-        ).reshape(LAYERS, -1).astype(F32)
-        full_up_bias = jnp.concatenate(
-            [part[0, bias_cut:].reshape(LAYERS, -1) for part in bias_parts], 1
-        ).astype(F32)
+            .reshape(LAYERS, 3, shard_width),
+            2,
+        ).reshape(-1)
+        up_bias_part = own_part(up_bias, 1).reshape(-1)
+        bias_cut = qkv_bias_part.shape[0]
+        bias_size = bias_cut + up_bias_part.shape[0]
+        bias_piece = jnp.pad(
+            jnp.concatenate([qkv_bias_part, up_bias_part])[None],
+            ((0, BIAS_ROWS - 1), (0, features - bias_size)),
+        )
+        pieces = []
         for layer in range(LAYERS):
             qkv_view = (
                 qkv_weight[layer]
@@ -261,21 +381,66 @@
                 .transpose(2, 1, 3, 0)
                 .reshape(3, shard_width, features)
             )
-            qkv_full = jnp.concatenate(fetch(own_part(qkv_view, 1)), 1).reshape(-1, features)
-            out_full = jnp.concatenate(fetch(own_part(out_weight[layer], 0)), 0)
-            up_full = jnp.concatenate(fetch(own_part(up_weight[layer], 1)), 1)
-            down_full = jnp.concatenate(fetch(own_part(down_weight[layer], 0)), 0)
-            weights.append((qkv_full, out_full, up_full, down_full))
-
-        head_here = weights[0][1].shape[0] // head_dim
-        part_width = shard_width // Y
+            pieces.append(
+                (
+                    own_part(qkv_view, 1).reshape(-1, features),
+                    own_part(out_weight[layer], 0),
+                    own_part(up_weight[layer], 1).T,
+                    own_part(down_weight[layer], 0),
+                )
+            )
+        weights = []
+        for layer in range(LAYERS):
+            qkv_piece, out_piece, up_piece, down_piece = pieces[layer]
+            if layer == 0:
+                with_bias, out_got = fetch(
+                    jnp.concatenate([qkv_piece, bias_piece, out_piece]),
+                    (3 * part_width + BIAS_ROWS, part_width),
+                )
+                qkv_got = with_bias[:, :, : 3 * part_width]
+                bias_got = with_bias[:, :, 3 * part_width, :bias_size].astype(F32)
+                up_got, down_got = fetch(
+                    jnp.concatenate([up_piece, down_piece]), (hidden_part, hidden_part)
+                )
+            else:
+                qkv_got, out_got, up_got, down_got = fetch(
+                    jnp.concatenate([qkv_piece, out_piece, up_piece, down_piece]),
+                    (3 * part_width, part_width, hidden_part, hidden_part),
+                )
+            weights.append(
+                (
+                    qkv_got.reshape(Y, shards, 3, part_width, features)
+                    .transpose(2, 1, 0, 3, 4)
+                    .reshape(-1, features),
+                    out_got.swapaxes(0, 1).reshape(-1, features),
+                    up_got.reshape(-1, features),
+                    down_got.reshape(-1, features),
+                )
+            )
+        full_qkv_bias = (
+            bias_got[:, :, :bias_cut]
+            .reshape(Y, shards, LAYERS, 3, part_width)
+            .transpose(2, 3, 1, 0, 4)
+            .reshape(LAYERS, -1)
+        )
+        full_up_bias = (
+            bias_got[:, :, bias_cut:]
+            .reshape(Y, shards, LAYERS, hidden_part)
+            .transpose(2, 0, 1, 3)
+            .reshape(LAYERS, -1)
+        )
+
+        head_here = shards * shard_width // (xs * head_dim)
+        x_width = shard_width // xs
         element = jnp.arange(head_here) * head_dim
-        shard_step = element // shard_width
-        y_step = element % shard_width // part_width
-        shard_z = x_at * OWN + (z_at + shard_step) % OWN
-        y_true = (y_at + y_step) % Y
-        head_ids = ((shard_z * C + c_at) * shard_width + y_true * part_width) // head_dim
-        slopes = jnp.exp2(-8.0 * (head_ids + 1).astype(F32) / HEADS)
+        shard_step = element // x_width
+        y_true = (y_at + element % x_width // part_width) % Y
+        if cut_by_x:
+            shard_z, x_start = shard_step, x_at * x_width
+        else:
+            shard_z, x_start = x_at * OWN + (z_at + shard_step) % OWN, 0
+        column = (shard_z * C + c_at) * shard_width + x_start + y_true * part_width
+        slopes = jnp.exp2(-8.0 * (column // head_dim + 1).astype(F32) / HEADS)
 
         slot = y_at * Z + z_at
         sequence = seq_deal[slot]
@@ -307,20 +472,17 @@
             return (block[:, None] * held_len + jnp.arange(held_len)[None, :]).reshape(-1)
 
         own_position = positions(x_at, c_at)
-        position = jnp.concatenate(
+        places = jnp.concatenate(
             [
-                positions((x_at + x_step) % X, (c_at + c_step) % C)
+                ((c_at + c_step) % C * blocks + jnp.arange(blocks)) * X + (x_at + x_step) % X
                 for x_step in range(X)
                 for c_step in range(C)
             ]
         )
+        length_row = length[None]
         keep_rows = (own_position < length).astype(F32)[:, None]
         residual = deal(tokens).astype(F32) * keep_rows
         grad_rows = deal(cotangent).astype(F32) * keep_rows
-
-        def split_heads(rows):
-            cut = rows.reshape(seq_len, 3, head_here, head_dim)
-            return cut[:, 0], cut[:, 1], cut[:, 2]
 
         saved = []
         for layer in range(LAYERS):
@@ -331,11 +493,12 @@
             before = residual
             first_norm = spread(layer_norm(before, gains[0], shifts[0]).astype(BF16))
             mixed = (dot(first_norm, qkv_full, 1, 1) + full_qkv_bias[layer]).astype(BF16)
-            context, log_total = attend_forward(*split_heads(mixed), slopes, position, length)
-            context = context.reshape(seq_len, -1)
+            context, log_total = attend_forward(
+                mixed, places, length_row, slopes, head_here, head_dim
+            )
             middle = before + (collect(context, out_full, 0) + biases[0])
             second_norm = spread(layer_norm(middle, gains[1], shifts[1]).astype(BF16))
-            upward = dot(second_norm, up_full, 1, 0) + full_up_bias[layer]
+            upward = dot(second_norm, up_full, 1, 1) + full_up_bias[layer]
             activated, act_slope = gelu_pair(upward)
             activated = activated.astype(BF16)
             act_slope = act_slope.astype(BF16)
@@ -400,15 +563,17 @@
         small = [None] * LAYERS
         bias_grads = [None] * LAYERS
 
-        def cut_rows(array, pieces):
-            size = array.shape[0] // pieces
-            return [array[at * size : (at + 1) * size] for at in range(pieces)]
-
-        def cut_columns(array, pieces):
-            size = array.shape[1] // pieces
-            return [array[:, at * size : (at + 1) * size] for at in range(pieces)]
-
-        pieces = OWN * Y
+        def hidden_grad(left_side, right_side):
+            size = left_side.shape[1] // Y
+            return sum_over_y(
+                [
+                    dot(left_side[:, at * size : (at + 1) * size], right_side, 0, 0).reshape(
+                        shards, hidden_part, features
+                    )
+                    for at in range(Y)
+                ]
+            )
+
         for layer in reversed(range(LAYERS)):
             qkv_full, out_full, up_full, down_full = weights[layer]
             (
@@ -427,9 +592,12 @@
             down_bias_grad = jnp.sum(down_grad, 0, dtype=F32)
             down_rows = spread(down_grad)
             up_grad = (dot(down_rows, down_full, 1, 1) * act_slope.astype(F32)).astype(BF16)
-            norm_grad = collect(up_grad, up_full, 1)
-            grad_down = settle(cut_rows(dot(activated, down_rows, 0, 0), pieces))
-            grad_up = settle(cut_columns(dot(second_norm, up_grad, 0, 0), pieces))
+            norm_grad = collect(up_grad, up_full, 0)
+            hidden = settle(
+                jnp.concatenate(
+                    [hidden_grad(activated, down_rows), hidden_grad(up_grad, second_norm)], 1
+                )
+            )
             up_bias_grad = jnp.sum(up_grad, 0, dtype=F32)
             added, second_gain, second_shift = norm_back(middle, gains[1], norm_grad)
             grad_rows = grad_rows + added
@@ -437,32 +605,60 @@
             out_bias_grad = jnp.sum(attn_grad, 0, dtype=F32)
             attn_rows = spread(attn_grad)
             context_grad = dot(attn_rows, out_full, 1, 1).astype(BF16)
-            grad_out = settle(cut_rows(dot(context, attn_rows, 0, 0), pieces))
+            grad_out = dot(context, attn_rows, 0, 0).astype(BF16)
             mixed_grad = attend_backward(
-                *split_heads(mixed),
+                mixed,
+                context,
+                context_grad,
+                log_total,
+                places,
+                length_row,
                 slopes,
-                position,
-                length,
-                log_total,
-                context_grad.reshape(seq_len, head_here, head_dim),
-            ).reshape(seq_len, -1)
-            grad_qkv = dot(mixed_grad, first_norm, 0, 0).reshape(3, -1, features)
-            grad_qkv = settle(cut_columns(grad_qkv, pieces))
+                head_here,
+                head_dim,
+            )
+            grad_qkv = dot(mixed_grad, first_norm, 0, 0).astype(BF16)
             qkv_bias_grad = jnp.sum(mixed_grad, 0, dtype=F32)
+            bias_grads[layer] = (
+                qkv_bias_grad.reshape(3, shards, Y, part_width)
+                .transpose(2, 1, 0, 3)
+                .reshape(Y, shards, -1),
+                up_bias_grad.reshape(Y, shards, -1),
+            )
+            parts = [
+                grad_out.reshape(shards, Y, part_width, features).swapaxes(0, 1),
+                grad_qkv.reshape(3, shards, Y, part_width, features)
+                .transpose(2, 1, 0, 3, 4)
+                .reshape(Y, shards, -1, features),
+            ]
+            if layer == 0:
+                bias_row = jnp.concatenate(
+                    [entry[0] for entry in bias_grads] + [entry[1] for entry in bias_grads], 2
+                ).astype(BF16)
+                parts.append(
+                    jnp.pad(
+                        bias_row[:, :, None],
+                        ((0, 0), (0, 0), (0, BIAS_ROWS - 1), (0, features - bias_size)),
+                    )
+                )
+            parts = jnp.concatenate(parts, 2)
+            attention = settle(sum_over_y(parts))
             norm_grad = collect(mixed_grad, qkv_full, 0)
             added, first_gain, first_shift = norm_back(before, gains[0], norm_grad)
             grad_rows = grad_rows + added
             grad_qkv = (
-                grad_qkv.transpose(3, 0, 2, 1)
+                attention[:, part_width : 4 * part_width]
+                .reshape(splits, 3, part_width, features)
+                .transpose(3, 0, 2, 1)
                 .reshape(features, shard_heads, head_dim, 3)
                 .transpose(0, 1, 3, 2)
                 .reshape(features, -1)
             )
             outputs[layer] = (
                 grad_qkv.astype(F32),
-                grad_out.reshape(-1, features).astype(F32),
-                grad_up.transpose(1, 0, 2).reshape(features, -1).astype(F32),
-                grad_down.reshape(-1, features).astype(F32),
+                attention[:, :part_width].reshape(-1, features).astype(F32),
+                hidden[:, hidden_part:].reshape(-1, features).T.astype(F32),
+                hidden[:, :hidden_part].reshape(-1, features).astype(F32),
             )
             small[layer] = jnp.stack(
                 [
@@ -474,26 +670,20 @@
                     down_bias_grad,
                 ]
             )
-            bias_grads[layer] = (qkv_bias_grad.reshape(3, pieces, -1), up_bias_grad)
-
-        bias_pieces = []
-        for at in range(pieces):
-            row = [bias_grads[layer][0][:, at].reshape(-1) for layer in range(LAYERS)]
-            row += [
-                bias_grads[layer][1].reshape(pieces, -1)[at] for layer in range(LAYERS)
-            ]
-            bias_pieces.append(jnp.concatenate(row)[None])
-        bias_total = settle(bias_pieces, F32)[:, 0]
+        bias_total = attention[:, 4 * part_width, :bias_size].astype(F32)
         grad_qkv_bias = (
             bias_total[:, :bias_cut]
-            .reshape(Y, LAYERS, 3, part_width)
+            .reshape(splits, LAYERS, 3, part_width)
             .transpose(1, 2, 0, 3)
             .reshape(LAYERS, 3, shard_heads, head_dim)
             .transpose(0, 2, 1, 3)
             .reshape(LAYERS, -1)
         )
         grad_up_bias = (
-            bias_total[:, bias_cut:].reshape(Y, LAYERS, -1).transpose(1, 0, 2).reshape(LAYERS, -1)
+            bias_total[:, bias_cut:]
+            .reshape(splits, LAYERS, -1)
+            .transpose(1, 0, 2)
+            .reshape(LAYERS, -1)
         )
 
         total = jnp.concatenate(small)
@@ -565,37 +755,44 @@
 
 
 def solution(mesh):
+    data_size, tensor_size = mesh.shape["dp"], mesh.shape["tensor"]
+    x_size = math.isqrt(data_size)
+    fine = Mesh(
+        mesh.devices.reshape(data_size // x_size, x_size, tensor_size // 2, 2),
+        ("y", "x", "z", "c"),
+    )
+    data, tensor = ("y", "x"), ("z", "c")
     placed = (
-        P(None, "dp", None),
-        P(None, "dp", None),
+        P(None, data, None),
+        P(None, data, None),
         P(),
         P(),
         P(),
         P(),
-        P(None, None, "tensor"),
-        P(None, "tensor"),
-        P(None, "tensor", None),
+        P(None, None, tensor),
+        P(None, tensor),
+        P(None, tensor, None),
         P(),
-        P(None, None, "tensor"),
-        P(None, "tensor"),
-        P(None, "tensor", None),
+        P(None, None, tensor),
+        P(None, tensor),
+        P(None, tensor, None),
     )
     return jax.shard_map(
-        make_body(mesh.shape["dp"], mesh.shape["tensor"]),
-        mesh=mesh,
+        make_body(data_size, tensor_size),
+        mesh=fine,
         in_specs=placed,
         out_specs=(
-            P("dp", None, "tensor", None),
-            P(None, "dp", None),
+            P(data, None, tensor, None),
+            P(None, data, None),
             P(),
             P(),
-            P(None, None, "tensor"),
-            P(None, "tensor"),
-            P(None, "tensor", None),
+            P(None, None, tensor),
+            P(None, tensor),
+            P(None, tensor, None),
             P(),
-            P(None, None, "tensor"),
-            P(None, "tensor"),
-            P(None, "tensor", None),
+            P(None, None, tensor),
+            P(None, tensor),
+            P(None, tensor, None),
         ),
         check_vma=False,
     )

time: 1000 us -> 770 us (0.77)
  starting transfers between devices: 229 us -> 85 us
  matrix products: 179 us -> 80.8 us
  other arithmetic: 150 us -> 67.1 us
  Pallas kernels: 0 us -> 35.4 us
  waiting for transfers between devices: 350 us -> 377 us
  local copies, waits for them, and re-layouts: 63.3 us -> 76.2 us
  between operations: 24.6 us -> 37.3 us
    ppermute x165 -> x89, starting transfers between devices: 229 us -> 84.3 us  [send(): return lax.ppermute(value, AXES, pairs)]
    dot_general x12 -> x0, matrix products: 81.8 us -> none  [the longest x2 22.3 us: attend_backward(): jnp.einsum('qhd,khd->hqk', context_grad, values, preferred_element_type=F32)]
    all_gather x0 -> x7, waiting for transfers between devices: none -> 65.3 us  [the longest x4 55.2 us: settle(): full = lax.all_gather(low, ('y', 'x'), axis=0)]
    convert_element_type x29 -> x8, other arithmetic: 47.9 us -> 6.8 us  [the longest x6 6.78 us: sum_over_y(): return here.astype(BF16)]
    ppermute x165 -> x89, waiting for transfers between devices: 350 us -> 310 us  [send(): return lax.ppermute(value, AXES, pairs)]
    pallas_call x0 -> x4, Pallas kernels: none -> 35.4 us  [the longest x2 21.8 us: attend_backward(): pl.pallas_call(functools.partial(backward_kernel, heads, width, block), o...]
    dot_general x32 -> x36, matrix products: 97 us -> 80.8 us  [dot(): lax.dot_general(left_side, right_side, (((left_dim,), (right_dim,)), ((),...]
    reduce_sum x2 -> x0, other arithmetic: 16 us -> none  [attend_forward(): jnp.sum(jnp.exp(scores - highest), -1, keepdims=True)]
  transfers between devices with their start and end apart: 165 -> 100, of which waited for: 57 -> 39; matrix products, arithmetic and copies ran while one was open for 35% -> 25% of each run, Pallas kernels for 0% -> 2%
where the time goes in v2:
time: 770 us; the launch traced here: 758 us
  waiting for transfers between devices  377 us (49%)
  starting transfers between devices  85 us (11%)
  matrix products  80.8 us (10%)
  local copies, waits for them, and re-layouts  76.2 us (10%)
  other arithmetic  67.1 us (9%)
  between operations  37.3 us (5%)
  Pallas kernels  35.4 us (5%)
    ppermute x89, waiting for transfers between devices, send(): return lax.ppermute(value, AXES, pairs)  310 us
    ppermute x89, starting transfers between devices, send(): return lax.ppermute(value, AXES, pairs)  84.3 us
    dot_general x36, matrix products, dot(): lax.dot_general(left_side, right_side, (((left_dim,), (right_dim,)), ((),...  80.8 us
    all_gather x4, waiting for transfers between devices, settle(): full = lax.all_gather(low, ('y', 'x'), axis=0)  55.2 us
    pallas_call x2, Pallas kernels, attend_backward(): pl.pallas_call(functools.partial(backward_kernel, heads, width, block), o...  21.8 us
  transfers between devices with their start and end apart: 100, of which 39 were waited for; matrix products, arithmetic and copies ran while one was open for 25% of the time, Pallas kernels for 2%

profile of v2, /device:TPU:0, one launch (start us, length us, event | category | flops | bytes accessed | tf_op | source)
XLA Modules:
  0.0 758.4 jit_solution(7181658459446138549)
XLA Ops:
  38.7 6.9 all-gather.15.cloned.1.call-done
  63.9 10.3 %collective-permute-done.5 = bf16[4,32,1024]{2,1,0:T(8,128)(2,1)} collective-permute-done((bf16[4,32,1024]{2,1,0:T(8,128)(2,1)S(1)}, bf16[4,32,1024]{2,1,0:T(8,128)(2,1)}, u32[]{:S(2)}, u32[]{:S(2)}) %collective-permute-start.5) | collective-permute-done | bytes 262176 | tf_op jit(solution)/shard_map/ppermute | solution.py:213
  80.9 6.8 shard_map.212
  119.0 6.7 collective-permute-done.10
  130.1 19.7 %collective-permute-done.12 = bf16[4,128,1024]{2,1,0:T(8,128)(2,1)} collective-permute-done((bf16[4,128,1024]{2,1,0:T(8,128)(2,1)}, bf16[4,128,1024]{2,1,0:T(8,128)(2,1)}, u32[]{:S(2)}, u32[]{:S(2)}) %collective-permute-start.12) | collective-permute-done | bytes 1048608 | tf_op jit(solution)/shard_map/ppermute | solution.py:213
  151.3 7.1 multiply_convert_fusion.3
  163.2 12.7 %collective-permute-done.15 = bf16[256,1024]{1,0:T(8,128)(2,1)S(1)} collective-permute-done((bf16[256,1024]{1,0:T(8,128)(2,1)S(1)}, bf16[256,1024]{1,0:T(8,128)(2,1)S(1)}, u32[]{:S(2)}, u32[]{:S(2)}) %collective-permute-start.15) | collective-permute-done | bytes 524320 | tf_op jit(solution)/shard_map/ppermute | solution.py:213
  192.2 20.5 %collective-permute-done.21 = bf16[4,32,1024]{2,1,0:T(8,128)(2,1)} collective-permute-done((bf16[4,32,1024]{2,1,0:T(8,128)(2,1)}, bf16[4,32,1024]{2,1,0:T(8,128)(2,1)}, u32[]{:S(2)}, u32[]{:S(2)}) %collective-permute-start.21) | collective-permute-done | bytes 262176 | tf_op jit(solution)/shard_map/ppermute | solution.py:213
  218.6 6.8 shard_map.213
  232.2 9.9 %collective-permute-done.23 = bf16[256,1024]{1,0:T(8,128)(2,1)S(1)} collective-permute-done((bf16[256,1024]{1,0:T(8,128)(2,1)S(1)}, bf16[256,1024]{1,0:T(8,128)(2,1)S(1)}, u32[]{:S(2)}, u32[]{:S(2)}) %collective-permute-start.23) | collective-permute-done | bytes 524320 | tf_op jit(solution)/shard_map/ppermute | solution.py:213
  245.2 12.8 %collective-permute-done.26 = bf16[256,1024]{1,0:T(8,128)(2,1)S(1)} collective-permute-done((bf16[256,1024]{1,0:T(8,128)(2,1)S(1)}, bf16[256,1024]{1,0:T(8,128)(2,1)S(1)}, u32[]{:S(2)}, u32[]{:S(2)}) %collective-permute-start.26) | collective-permute-done | bytes 524320 | tf_op jit(solution)/shard_map/ppermute | solution.py:213
  258.0 9.5 %collective-permute-done.40 = bf16[256,1024]{1,0:T(8,128)(2,1)S(1)} collective-permute-done((bf16[256,1024]{1,0:T(8,128)(2,1)S(1)}, bf16[256,1024]{1,0:T(8,128)(2,1)S(1)}, u32[]{:S(2)}, u32[]{:S(2)}) %collective-permute-start.40) | collective-permute-done | bytes 524320 | tf_op jit(solution)/shard_map/ppermute | solution.py:213
  268.2 9.4 %collective-permute-done.29 = bf16[4,128,1024]{2,1,0:T(8,128)(2,1)S(1)} collective-permute-done((bf16[4,128,1024]{2,1,0:T(8,128)(2,1)S(1)}, bf16[4,128,1024]{2,1,0:T(8,128)(2,1)S(1)}, u32[]{:S(2)}, u32[]{:S(2)}) %collective-permute-start.29) | collective-permute-done | bytes 1048608 | tf_op jit(solution)/shard_map/ppermute | solution.py:213
  281.4 6.7 fusion.106
  297.0 10.8 %collective-permute-done.43 = bf16[256,1024]{1,0:T(8,128)(2,1)S(1)} collective-permute-done((bf16[256,1024]{1,0:T(8,128)(2,1)S(1)}, bf16[256,1024]{1,0:T(8,128)(2,1)S(1)}, u32[]{:S(2)}, u32[]{:S(2)}) %collective-permute-start.43) | collective-permute-done | bytes 524320 | tf_op jit(solution)/shard_map/ppermute | solution.py:213
  308.5 10.2 %collective-permute-done.31 = bf16[256,1024]{1,0:T(8,128)(2,1)S(1)} collective-permute-done((bf16[256,1024]{1,0:T(8,128)(2,1)S(1)}, bf16[256,1024]{1,0:T(8,128)(2,1)S(1)}, u32[]{:S(2)}, u32[]{:S(2)}) %collective-permute-start.31) | collective-permute-done | bytes 524320 | tf_op jit(solution)/shard_map/ppermute | solution.py:213
  322.0 13.1 %collective-permute-done.46 = bf16[256,1024]{1,0:T(8,128)(2,1)S(1)} collective-permute-done((bf16[256,1024]{1,0:T(8,128)(2,1)S(1)}, bf16[256,1024]{1,0:T(8,128)(2,1)S(1)}, u32[]{:S(2)}, u32[]{:S(2)}) %collective-permute-start.46) | collective-permute-done | bytes 524320 | tf_op jit(solution)/shard_map/ppermute | solution.py:213
  337.8 11.1 %shard_map.214 = bf16[1024,768]{1,0:T(8,128)(2,1)S(1)} custom-call(s32[4]{0:T(128)S(1)} %pad_add_fusion.places, s32[1]{0:T(128)} %dynamic_slice.127.length, f32[4]{0:T(128)S(1)} %multiply_exponential_fusion.slopes, bf16[1024,768]{1,0:T(8,128)(2,1)S(1)} %add_convert_fusion.2.mixed, bf16[1024,256]{1,0:T(8,128)(2,1)S(1)} %get-tuple-element.16.context, ...), custom_call_target="tpu_custom_call" | custom-call | flops 2684354560 | bytes 6291456 | tf_op jit(solution)/shard_map/pallas_call | solution.py:179
  356.5 9.7 %collective-permute-done.49 = bf16[256,1024]{1,0:T(8,128)(2,1)S(1)} collective-permute-done((bf16[256,1024]{1,0:T(8,128)(2,1)S(1)}, bf16[256,1024]{1,0:T(8,128)(2,1)S(1)}, u32[]{:S(2)}, u32[]{:S(2)}) %collective-permute-start.49) | collective-permute-done | bytes 524320 | tf_op jit(solution)/shard_map/ppermute | solution.py:213
  388.7 6.7 fusion.107
  398.0 27.8 %collective-permute-done.84 = bf16[4,128,1024]{2,1,0:T(8,128)(2,1)S(1)} collective-permute-done((bf16[4,128,1024]{2,1,0:T(8,128)(2,1)S(1)}, bf16[4,128,1024]{2,1,0:T(8,128)(2,1)S(1)}, u32[]{:S(2)}, u32[]{:S(2)}) %collective-permute-start.84) | collective-permute-done | bytes 1048608 | tf_op jit(solution)/shard_map/ppermute | solution.py:213
  436.1 10.3 %collective-permute-done.55 = bf16[256,1024]{1,0:T(8,128)(2,1)S(1)} collective-permute-done((bf16[256,1024]{1,0:T(8,128)(2,1)S(1)}, bf16[256,1024]{1,0:T(8,128)(2,1)S(1)}, u32[]{:S(2)}, u32[]{:S(2)}) %collective-permute-start.55) | collective-permute-done | bytes 524320 | tf_op jit(solution)/shard_map/ppermute | solution.py:213
  453.1 9.3 %collective-permute-done.58 = bf16[256,1024]{1,0:T(8,128)(2,1)} collective-permute-done((bf16[256,1024]{1,0:T(8,128)(2,1)}, bf16[256,1024]{1,0:T(8,128)(2,1)}, u32[]{:S(2)}, u32[]{:S(2)}) %collective-permute-start.58) | collective-permute-done | bytes 524320 | tf_op jit(solution)/shard_map/ppermute | solution.py:213
  467.0 10.7 %shard_map.215 = bf16[1024,768]{1,0:T(8,128)(2,1)S(1)} custom-call(s32[4]{0:T(128)S(1)} %pad_add_fusion.places, s32[1]{0:T(128)} %dynamic_slice.127.length, f32[4]{0:T(128)S(1)} %multiply_exponential_fusion.slopes, bf16[1024,768]{1,0:T(8,128)(2,1)S(1)} %copy-done.3, bf16[1024,256]{1,0:T(8,128)(2,1)S(1)} %get-tuple-element.15.context, ...), custom_call_target="tpu_custom_call" | custom-call | flops 2684354560 | bytes 6291456 | tf_op jit(solution)/shard_map/pallas_call | solution.py:179
  486.5 25.1 %collective-permute-done.83 = bf16[4,136,1024]{2,1,0:T(8,128)(2,1)S(1)} collective-permute-done((bf16[4,136,1024]{2,1,0:T(8,128)(2,1)S(1)}, bf16[4,136,1024]{2,1,0:T(8,128)(2,1)S(1)}, u32[]{:S(2)}, u32[]{:S(2)}) %collective-permute-start.83) | collective-permute-done | bytes 1114144 | tf_op jit(solution)/shard_map/ppermute | solution.py:213
  523.4 18.9 %collective-permute-done.86 = bf16[4,128,1024]{2,1,0:T(8,128)(2,1)S(1)} collective-permute-done((bf16[4,128,1024]{2,1,0:T(8,128)(2,1)S(1)}, bf16[4,128,1024]{2,1,0:T(8,128)(2,1)S(1)}, u32[]{:S(2)}, u32[]{:S(2)}) %collective-permute-start.86) | collective-permute-done | bytes 1048608 | tf_op jit(solution)/shard_map/ppermute | solution.py:213
  542.6 20.4 %collective-permute-done.85 = bf16[4,128,1024]{2,1,0:T(8,128)(2,1)S(1)} collective-permute-done((bf16[4,128,1024]{2,1,0:T(8,128)(2,1)S(1)}, bf16[4,128,1024]{2,1,0:T(8,128)(2,1)S(1)}, u32[]{:S(2)}, u32[]{:S(2)}) %collective-permute-start.85) | collective-permute-done | bytes 1048608 | tf_op jit(solution)/shard_map/ppermute | solution.py:213
  576.6 11.0 %collective-permute-done.61 = bf16[256,1024]{1,0:T(8,128)(2,1)} collective-permute-done((bf16[256,1024]{1,0:T(8,128)(2,1)}, bf16[256,1024]{1,0:T(8,128)(2,1)}, u32[]{:S(2)}, u32[]{:S(2)}) %collective-permute-start.61) | collective-permute-done | bytes 524320 | tf_op jit(solution)/shard_map/ppermute | solution.py:213
  628.7 12.6 %collective-permute-start.79 = (f32[12,1024]{1,0:T(8,128)S(1)}, f32[12,1024]{1,0:T(8,128)S(1)}, u32[]{:S(2)}, u32[]{:S(2)}) collective-permute-start(f32[12,1024]{1,0:T(8,128)S(1)} %add.904), channel_id=1, source_target_pairs={{0,8},{1,9},{2,10},{3,11},{4,12},{5,13},{6,14},{7,15},{8,0},{9,1},... | collective-permute-start | bytes 147464 | tf_op jit(solution)/shard_map/ppermute | solution.py:213
  668.2 8.5 %all-gather.27.cloned.1.call-done = bf16[1024,1024]{1,0:T(8,128)(2,1)} async-done(((bf16[256,1024]{1,0:T(8,128)(2,1)}), bf16[1024,1024]{1,0:T(8,128)(2,1)}) %all-gather.27.cloned.1.call-update) | async-done | bytes 2097168 | tf_op jit(solution)/shard_map/all_gather | solution.py:329
  687.5 18.2 %all-gather.21.cloned.1.call-done = bf16[544,1024]{1,0:T(8,128)(2,1)} async-done(((bf16[136,1024]{1,0:T(8,128)(2,1)}), bf16[544,1024]{1,0:T(8,128)(2,1)}) %all-gather.21.cloned.1.call-update) | async-done | bytes 1114128 | tf_op jit(solution)/shard_map/all_gather | solution.py:329
  714.3 28.5 %all-gather.25.cloned.1.call-done = bf16[1024,1024]{1,0:T(8,128)(2,1)} async-done(((bf16[256,1024]{1,0:T(8,128)(2,1)}), bf16[1024,1024]{1,0:T(8,128)(2,1)}) %all-gather.25.cloned.1.call-update) | async-done | bytes 2097168 | tf_op jit(solution)/shard_map/all_gather | solution.py:329
  (620 shorter events, 312.3 us)
Async XLA Ops:
  7.2 38.4 %all-gather.15.cloned.1.call-start = ((), (), s32[]{:S(2)}) async-start(), calls=%async_computation.8 | async-start | bytes 1392640 | tf_op jit(solution)/shard_map/all_gather | solution.py:277
  13.8 80.5 %all-gather.17.cloned.1.call-start = ((), (), s32[]{:S(2)}) async-start(), calls=%async_computation.9 | async-start | bytes 2621440 | tf_op jit(solution)/shard_map/all_gather | solution.py:277
  18.5 85.8 %collective-permute-start.38 = (bf16[256,1024]{1,0:T(8,128)(2,1)}, bf16[256,1024]{1,0:T(8,128)(2,1)}, u32[]{:S(2)}, u32[]{:S(2)}) collective-permute-start(bf16[256,1024]{1,0:T(8,128)(2,1)} %dynamic-slice_bitcast_fusion), channel_id=1, source_target_pairs={{0,16},{2,18},{4,20},{6,22},{8,24},{10,26},{12,28},{14,30},{17,1},... | collective-permute-start | bytes 1572872 | tf_op jit(solution)/shard_map/ppermute | solution.py:213
  31.6 149.8 %all-gather.19.cloned.1.call-start = ((), (), s32[]{:S(2)}) async-start(), calls=%async_computation.10 | async-start | bytes 3932160 | tf_op jit(solution)/shard_map/all_gather | solution.py:277
  47.8 27.5 %collective-permute-start.4 = (bf16[4,104,1024]{2,1,0:T(8,128)(2,1)}, bf16[4,104,1024]{2,1,0:T(8,128)(2,1)S(1)}, u32[]{:S(2)}, u32[]{:S(2)}) collective-permute-start(bf16[4,104,1024]{2,1,0:T(8,128)(2,1)} %get-tuple-element.100), channel_id=1, source_target_pairs={{0,16},{1,17},{2,18},{3,19},{4,20},{5,21},{6,22},{7,23},{8,24},{9,... | collective-permute-start | bytes 2555912 | tf_op jit(solution)/shard_map/ppermute | solution.py:213
  102.2 26.4 %collective-permute-start.13 = (bf16[4,128,1024]{2,1,0:T(8,128)(2,1)}, bf16[4,128,1024]{2,1,0:T(8,128)(2,1)}, u32[]{:S(2)}, u32[]{:S(2)}) collective-permute-start(bf16[4,128,1024]{2,1,0:T(8,128)(2,1)} %get-tuple-element.96), channel_id=1, source_target_pairs={{0,16},{1,17},{2,18},{3,19},{4,20},{5,21},{6,22},{7,23},{8,24},{9,... | collective-permute-start | bytes 3145736 | tf_op jit(solution)/shard_map/ppermute | solution.py:213
  103.7 46.1 %collective-permute-start.12 = (bf16[4,128,1024]{2,1,0:T(8,128)(2,1)}, bf16[4,128,1024]{2,1,0:T(8,128)(2,1)}, u32[]{:S(2)}, u32[]{:S(2)}) collective-permute-start(bf16[4,128,1024]{2,1,0:T(8,128)(2,1)} %get-tuple-element.97), channel_id=1, source_target_pairs={{0,16},{1,17},{2,18},{3,19},{4,20},{5,21},{6,22},{7,23},{8,24},{9,... | collective-permute-start | bytes 3145736 | tf_op jit(solution)/shard_map/ppermute | solution.py:213
  118.8 446.1 %reduce-scatter.7.cloned.1.call-start = ((), (), s32[]{:S(2)}) async-start(), calls=%async_computation.5 | async-start | bytes 1310720 | tf_op jit(solution)/shard_map/reduce_scatter | solution.py:326
  119.0 32.3 %collective-permute-start.9 = (bf16[256,1024]{1,0:T(8,128)(2,1)}, bf16[256,1024]{1,0:T(8,128)(2,1)S(1)}, u32[]{:S(2)}, u32[]{:S(2)}) collective-permute-start(bf16[256,1024]{1,0:T(8,128)(2,1)} %add_convert_fusion.17), channel_id=1, source_target_pairs={{0,1},{1,0},{2,3},{3,2},{4,5},{5,4},{6,7},{7,6},{8,9},{9,8},{10,11... | collective-permute-start | bytes 1572872 | tf_op jit(solution)/shard_map/ppermute | solution.py:213
  187.6 26.2 %collective-permute-start.20 = (bf16[4,96,1024]{2,1,0:T(8,128)(2,1)S(1)}, bf16[4,96,1024]{2,1,0:T(8,128)(2,1)}, u32[]{:S(2)}, u32[]{:S(2)}) collective-permute-start(bf16[4,96,1024]{2,1,0:T(8,128)(2,1)S(1)} %slice.518), channel_id=1, source_target_pairs={{0,16},{1,17},{2,18},{3,19},{4,20},{5,21},{6,22},{7,23},{8,24},{9,... | collective-permute-start | bytes 2359304 | tf_op jit(solution)/shard_map/ppermute | solution.py:213
  230.2 37.4 %collective-permute-start.28 = (bf16[4,128,1024]{2,1,0:T(8,128)(2,1)S(1)}, bf16[4,128,1024]{2,1,0:T(8,128)(2,1)S(1)}, u32[]{:S(2)}, u32[]{:S(2)}) collective-permute-start(bf16[4,128,1024]{2,1,0:T(8,128)(2,1)S(1)} %get-tuple-element.83), channel_id=1, source_target_pairs={{0,16},{1,17},{2,18},{3,19},{4,20},{5,21},{6,22},{7,23},{8,24},{9,... | collective-permute-start | bytes 3145736 | tf_op jit(solution)/shard_map/ppermute | solution.py:213
  231.7 45.9 %collective-permute-start.29 = (bf16[4,128,1024]{2,1,0:T(8,128)(2,1)S(1)}, bf16[4,128,1024]{2,1,0:T(8,128)(2,1)S(1)}, u32[]{:S(2)}, u32[]{:S(2)}) collective-permute-start(bf16[4,128,1024]{2,1,0:T(8,128)(2,1)S(1)} %get-tuple-element.82), channel_id=1, source_target_pairs={{0,16},{1,17},{2,18},{3,19},{4,20},{5,21},{6,22},{7,23},{8,24},{9,... | collective-permute-start | bytes 3145736 | tf_op jit(solution)/shard_map/ppermute | solution.py:213
  245.2 32.6 %collective-permute-start.25 = (bf16[256,1024]{1,0:T(8,128)(2,1)S(1)}, bf16[256,1024]{1,0:T(8,128)(2,1)S(1)}, u32[]{:S(2)}, u32[]{:S(2)}) collective-permute-start(bf16[256,1024]{1,0:T(8,128)(2,1)S(1)} %add_convert_fusion.13), channel_id=1, source_target_pairs={{0,1},{1,0},{2,3},{3,2},{4,5},{5,4},{6,7},{7,6},{8,9},{9,8},{10,11... | collective-permute-start | bytes 1572872 | tf_op jit(solution)/shard_map/ppermute | solution.py:213
  355.2 79.2 %collective-permute-start.88 = (bf16[4,128,1024]{2,1,0:T(8,128)(2,1)}, bf16[4,128,1024]{2,1,0:T(8,128)(2,1)}, u32[]{:S(2)}, u32[]{:S(2)}) collective-permute-start(bf16[4,128,1024]{2,1,0:T(8,128)(2,1)} %bitcast.187), channel_id=1, source_target_pairs={{0,16},{1,17},{2,18},{3,19},{4,20},{5,21},{6,22},{7,23},{8,24},{9,... | collective-permute-start | bytes 3145736 | tf_op jit(solution)/shard_map/ppermute | solution.py:213
  371.7 77.9 %collective-permute-start.87 = (bf16[4,128,1024]{2,1,0:T(8,128)(2,1)}, bf16[4,128,1024]{2,1,0:T(8,128)(2,1)}, u32[]{:S(2)}, u32[]{:S(2)}) collective-permute-start(bf16[4,128,1024]{2,1,0:T(8,128)(2,1)} %bitcast.185), channel_id=1, source_target_pairs={{0,16},{1,17},{2,18},{3,19},{4,20},{5,21},{6,22},{7,23},{8,24},{9,... | collective-permute-start | bytes 3145736 | tf_op jit(solution)/shard_map/ppermute | solution.py:213
  386.5 39.2 %collective-permute-start.84 = (bf16[4,128,1024]{2,1,0:T(8,128)(2,1)S(1)}, bf16[4,128,1024]{2,1,0:T(8,128)(2,1)S(1)}, u32[]{:S(2)}, u32[]{:S(2)}) collective-permute-start(bf16[4,128,1024]{2,1,0:T(8,128)(2,1)S(1)} %fusion.17), channel_id=1, source_target_pairs={{0,16},{1,17},{2,18},{3,19},{4,20},{5,21},{6,22},{7,23},{8,24},{9,... | collective-permute-start | bytes 3145736 | tf_op jit(solution)/shard_map/ppermute | solution.py:213
  397.6 33.1 %collective-permute-start.54 = (bf16[256,1024]{1,0:T(8,128)(2,1)}, bf16[256,1024]{1,0:T(8,128)(2,1)}, u32[]{:S(2)}, u32[]{:S(2)}) collective-permute-start(bf16[256,1024]{1,0:T(8,128)(2,1)} %slice.552), channel_id=1, source_target_pairs={{0,1},{1,0},{2,3},{3,2},{4,5},{5,4},{6,7},{7,6},{8,9},{9,8},{10,11... | collective-permute-start | bytes 1572872 | tf_op jit(solution)/shard_map/ppermute | solution.py:213
  427.2 138.5 %reduce-scatter.11.cloned.1.call-start = ((), (), s32[]{:S(2)}) async-start(), calls=%async_computation.7 | async-start | bytes 2621440 | tf_op jit(solution)/shard_map/reduce_scatter | solution.py:326
  452.8 123.8 %reduce-scatter.5.cloned.1.call-start = ((), (), s32[]{:S(2)}) async-start(), calls=%async_computation.4 | async-start | bytes 1392640 | tf_op jit(solution)/shard_map/reduce_scatter | solution.py:326
  484.9 26.7 %collective-permute-start.83 = (bf16[4,136,1024]{2,1,0:T(8,128)(2,1)S(1)}, bf16[4,136,1024]{2,1,0:T(8,128)(2,1)S(1)}, u32[]{:S(2)}, u32[]{:S(2)}) collective-permute-start(bf16[4,136,1024]{2,1,0:T(8,128)(2,1)S(1)} %slice_bitcast_fusion), channel_id=1, source_target_pairs={{0,16},{1,17},{2,18},{3,19},{4,20},{5,21},{6,22},{7,23},{8,24},{9,... | collective-permute-start | bytes 3342344 | tf_op jit(solution)/shard_map/ppermute | solution.py:213
  513.0 102.3 %reduce-scatter.9.cloned.1.call-start = ((), (), s32[]{:S(2)}) async-start(), calls=%async_computation.6 | async-start | bytes 2621440 | tf_op jit(solution)/shard_map/reduce_scatter | solution.py:326
  516.1 26.2 %collective-permute-start.86 = (bf16[4,128,1024]{2,1,0:T(8,128)(2,1)S(1)}, bf16[4,128,1024]{2,1,0:T(8,128)(2,1)S(1)}, u32[]{:S(2)}, u32[]{:S(2)}) collective-permute-start(bf16[4,128,1024]{2,1,0:T(8,128)(2,1)S(1)} %bitcast.465), channel_id=1, source_target_pairs={{0,16},{1,17},{2,18},{3,19},{4,20},{5,21},{6,22},{7,23},{8,24},{9,... | collective-permute-start | bytes 3145736 | tf_op jit(solution)/shard_map/ppermute | solution.py:213
  519.0 44.0 %collective-permute-start.85 = (bf16[4,128,1024]{2,1,0:T(8,128)(2,1)S(1)}, bf16[4,128,1024]{2,1,0:T(8,128)(2,1)S(1)}, u32[]{:S(2)}, u32[]{:S(2)}) collective-permute-start(bf16[4,128,1024]{2,1,0:T(8,128)(2,1)S(1)} %bitcast.464), channel_id=1, source_target_pairs={{0,16},{1,17},{2,18},{3,19},{4,20},{5,21},{6,22},{7,23},{8,24},{9,... | collective-permute-start | bytes 3145736 | tf_op jit(solution)/shard_map/ppermute | solution.py:213
  564.9 100.3 %all-gather.23.cloned.1.call-start = ((), (), s32[]{:S(2)}) async-start(), calls=%async_computation.12 | async-start | bytes 1310720 | tf_op jit(solution)/shard_map/all_gather | solution.py:329
  565.6 111.1 %all-gather.27.cloned.1.call-start = ((), (), s32[]{:S(2)}) async-start(), calls=%async_computation.14 | async-start | bytes 2621440 | tf_op jit(solution)/shard_map/all_gather | solution.py:329
  566.4 139.3 %all-gather.21.cloned.1.call-start = ((), (), s32[]{:S(2)}) async-start(), calls=%async_computation.11 | async-start | bytes 1392640 | tf_op jit(solution)/shard_map/all_gather | solution.py:329
  576.6 166.3 %all-gather.25.cloned.1.call-start = ((), (), s32[]{:S(2)}) async-start(), calls=%async_computation.13 | async-start | bytes 2621440 | tf_op jit(solution)/shard_map/all_gather | solution.py:329
  601.9 26.9 %collective-permute-start.35 = (bf16[2,1,2,32,1024]{4,3,2,0,1:T(8,128)(2,1)S(1)}, bf16[2,1,2,32,1024]{4,3,2,0,1:T(8,128)(2,1)}, u32[]{:S(2)}, u32[]{:S(2)}) collective-permute-start(bf16[2,1,2,32,1024]{4,3,2,0,1:T(8,128)(2,1)S(1)} %get-tuple-element.107), channel_id=1, source_target_pairs={{0,4},{1,5},{2,6},{3,7},{12,8},{13,9},{14,10},{15,11},{16,20},{17,... | collective-permute-start | bytes 786440 | tf_op jit(solution)/shard_map/ppermute | solution.py:213
  603.9 37.5 %collective-permute-start.34 = (bf16[2,1,2,32,1024]{4,3,2,0,1:T(8,128)(2,1)S(1)}, bf16[2,1,2,32,1024]{4,3,2,0,1:T(8,128)(2,1)}, u32[]{:S(2)}, u32[]{:S(2)}) collective-permute-start(bf16[2,1,2,32,1024]{4,3,2,0,1:T(8,128)(2,1)S(1)} %get-tuple-element.108), channel_id=1, source_target_pairs={{0,2},{1,3},{2,4},{3,5},{12,14},{13,15},{14,8},{15,9},{16,18},{17,... | collective-permute-start | bytes 786440 | tf_op jit(solution)/shard_map/ppermute | solution.py:213
  608.5 36.6 %collective-permute-start.70 = (bf16[256,1024]{1,0:T(8,128)(2,1)}, bf16[256,1024]{1,0:T(8,128)(2,1)S(1)}, u32[]{:S(2)}, u32[]{:S(2)}) collective-permute-start(bf16[256,1024]{1,0:T(8,128)(2,1)} %multiply_convert_fusion.4), channel_id=1, source_target_pairs={{1,17},{3,19},{5,21},{7,23},{9,25},{11,27},{13,29},{15,31},{16,0},... | collective-permute-start | bytes 1572872 | tf_op jit(solution)/shard_map/ppermute | solution.py:213
  615.4 31.1 %collective-permute-start.64 = (bf16[128,1024]{1,0:T(8,128)(2,1)S(1)}, bf16[128,1024]{1,0:T(8,128)(2,1)S(1)}, u32[]{:S(2)}, u32[]{:S(2)}) collective-permute-start(bf16[128,1024]{1,0:T(8,128)(2,1)S(1)} %constant_dynamic-slice_fusion.1), channel_id=1, source_target_pairs={{0,2},{1,3},{2,4},{3,5},{4,6},{5,7},{6,0},{7,1},{8,10},{9,11},{10,... | collective-permute-start | bytes 786440 | tf_op jit(solution)/shard_map/ppermute | solution.py:213
  615.4 31.1 %collective-permute-start.66 = (bf16[128,1024]{1,0:T(8,128)(2,1)S(1)}, bf16[128,1024]{1,0:T(8,128)(2,1)S(1)}, u32[]{:S(2)}, u32[]{:S(2)}) collective-permute-start(bf16[128,1024]{1,0:T(8,128)(2,1)S(1)} %constant_dynamic-slice_fusion.1), channel_id=1, source_target_pairs={{0,4},{1,5},{2,6},{3,7},{4,0},{5,1},{6,2},{7,3},{8,12},{9,13},{10,... | collective-permute-start | bytes 786440 | tf_op jit(solution)/shard_map/ppermute | solution.py:213
  (155 other events, 1606.9 us)
Sparse Core Ops, SparseCore 0:
  13.9 31.6 all-gather.14
  47.2 45.7 all-gather.16
  119.0 62.4 all-gather.18
  427.3 25.2 reduce-scatter.6
  455.4 42.5 reduce-scatter.10
  513.1 26.3 reduce-scatter.4
  565.0 42.0 reduce-scatter.8
  608.9 29.1 all-gather.22
  640.0 36.6 all-gather.26
  678.4 27.1 all-gather.20
  707.5 35.2 all-gather.24
